TPU v7x, 128 devices: a whole 4x4x4 slice. The times are simulated.
128 devices in a mesh: rollout: 16 (over y, x_lo, core), tensor: 8 (over x_hi, z).
Axes of the slice: x: 4 (x_hi: 2, x_lo: 2; x = x_hi * 2 + x_lo), y: 4, z: 4, core: 2. Of those that a mesh axis runs over, the one named last changes fastest.
Arguments:
- inputs: bfloat16 [4, 2048, 8192], P(None, 'rollout', 'tensor'), may hold values from -6 to 6
- w_query: bfloat16 [8192, 4096], P(None, 'tensor'), may hold values from -0.0625 to 0.0625
- w_keyval: bfloat16 [8192, 2, 1024], P(None, None, 'tensor'), may hold values from -0.0625 to 0.0625
- bias_query: float32 [4096], P('tensor'), may hold values from -3 to 3
- bias_keyval: float32 [2, 1024], P(None, 'tensor'), may hold values from -3 to 3
- factor_down: bfloat16 [128, 3, 64, 8192], P(('rollout', 'tensor')), may hold values from -0.0625 to 0.0625
- factor_up: bfloat16 [128, 64, 6144], P(('rollout', 'tensor')), may hold values from -0.75 to 0.75
- cache: bfloat16 [2, 2048, 128, 1024], P(None, 'rollout', None, 'tensor'), may hold values from -384 to 384
- lengths: int32 [2048], P('rollout'), may hold values from 1 to 128, as said below
- owners: int32 [3], replicated, may hold values from 0 to 127
Outputs:
- context: bfloat16 [4, 2048, 4096], P(None, 'rollout', 'tensor')
Inputs may be any that keep to these rules, and one draw needn't show every extreme that they name: `lengths`: in every draw one row has length 128.
All inputs are finite; a program needn't handle non-finite values.
Results may differ from a plain program's by a relative error of at most 0.0085.
The roundings to bfloat16 on the way count: a program that leaves them out, or rounds other values in their place, can miss the bound.
Values may be sent and summed in bfloat16 or wider, within the bound.
A program may use at most 128 MiB of HBM per device.

v0:
```python
import math

import jax
import jax.numpy as jnp
from jax import lax
from jax.sharding import PartitionSpec as P

HD = 128


def spread(shard, axis, root):
    mine = lax.axis_index(axis) == root
    return lax.psum(jnp.where(mine, shard, jnp.zeros_like(shard)), axis)


def rotate(vectors, positions):
    half_size = vectors.shape[-1] // 2
    frequency = jnp.exp(
        -(jnp.arange(half_size, dtype=jnp.float32) * (2.0 / vectors.shape[-1]))
        * math.log(1000000.0)
    )
    angles = positions.astype(jnp.float32)[:, None] * frequency[None, :]
    cosine = jnp.cos(angles)[:, None, :]
    sine = jnp.sin(angles)[:, None, :]
    leading = vectors[..., :half_size]
    trailing = vectors[..., half_size:]
    return jnp.concatenate(
        [leading * cosine - trailing * sine, trailing * cosine + leading * sine], axis=-1
    )


def body(
    inputs,
    w_query,
    w_keyval,
    bias_query,
    bias_keyval,
    factor_down,
    factor_up,
    cache,
    lengths,
    owners,
):
    tensor_size = lax.axis_size("tensor")
    column = lax.axis_index("tensor")
    query_width = w_query.shape[1]
    keyval_width = w_keyval.shape[2]
    heads_query = query_width // HD
    heads_keyval = keyval_width // HD
    group_size = heads_query // heads_keyval
    full_query = query_width * tensor_size
    full_keyval = keyval_width * tensor_size
    span_starts = [0, full_query, full_query + full_keyval]
    span_sizes = [full_query, full_keyval, full_keyval]
    local_widths = [query_width, keyval_width, keyval_width]
    base_parts = [w_query, w_keyval[:, 0], w_keyval[:, 1]]
    model_width = factor_down.shape[3]
    merged_parts = []
    for member in range(3):
        held = jnp.concatenate(
            [
                factor_down[0, member],
                factor_up[0, :, span_starts[member] : span_starts[member] + span_sizes[member]],
            ],
            axis=1,
        )
        owner_id = owners[member]
        held = spread(held, ("rollout", "tensor"), owner_id)
        down_part = held[:, :model_width]
        up_part = lax.dynamic_slice_in_dim(
            held[:, model_width:], column * local_widths[member], local_widths[member], 1
        )
        low_rank = lax.dot_general(
            down_part, up_part, (((0,), (0,)), ((), ())), preferred_element_type=jnp.float32
        )
        merged_parts.append(
            (base_parts[member].astype(jnp.float32) + low_rank).astype(jnp.bfloat16)
        )
    merged = jnp.concatenate(merged_parts, axis=1)
    bias_all = jnp.concatenate([bias_query, bias_keyval[0], bias_keyval[1]])
    step_count = inputs.shape[0]
    row_count = inputs.shape[1]

    def project(received):
        return jnp.dot(received, merged, preferred_element_type=jnp.float32)

    step_projections = [
        project(lax.all_gather(inputs[step_index], "tensor", axis=1, tiled=True))
        for step_index in range(step_count)
    ]
    cache_slots = cache.shape[2]
    cache_keys = cache[0].reshape(row_count, cache_slots, heads_keyval, HD)
    cache_values = cache[1].reshape(row_count, cache_slots, heads_keyval, HD)
    live_mask = jnp.arange(cache_slots, dtype=jnp.int32)[None, :] < lengths[:, None]
    score_scale = 1.0 / math.sqrt(HD)
    new_keys = []
    new_values = []
    outputs = []
    for step_index in range(step_count):
        positions = lengths + step_index
        projected_now = step_projections[step_index] + bias_all
        queries = rotate(
            projected_now[:, :query_width].reshape(row_count, heads_query, HD), positions
        ).astype(jnp.bfloat16)
        keys_now = rotate(
            projected_now[:, query_width : query_width + keyval_width].reshape(
                row_count, heads_keyval, HD
            ),
            positions,
        ).astype(jnp.bfloat16)
        values_now = (
            projected_now[:, query_width + keyval_width :]
            .reshape(row_count, heads_keyval, HD)
            .astype(jnp.bfloat16)
        )
        new_keys.append(keys_now)
        new_values.append(values_now)
        grouped = queries.reshape(row_count, heads_keyval, group_size, HD)
        cached_scores = (
            jnp.einsum("rkgd,rckd->rkgc", grouped, cache_keys, preferred_element_type=jnp.float32)
            * score_scale
        )
        cached_scores = jnp.where(live_mask[:, None, None, :], cached_scores, -1e30)
        recent_keys = jnp.stack(new_keys, axis=1)
        recent_values = jnp.stack(new_values, axis=1)
        recent_scores = (
            jnp.einsum("rkgd,rskd->rkgs", grouped, recent_keys, preferred_element_type=jnp.float32)
            * score_scale
        )
        scores = jnp.concatenate([cached_scores, recent_scores], axis=-1)
        row_max = jnp.max(scores, axis=-1, keepdims=True)
        weights = jnp.exp(scores - row_max)
        probs = (weights / jnp.sum(weights, axis=-1, keepdims=True)).astype(jnp.bfloat16)
        context = jnp.einsum(
            "rkgc,rckd->rkgd",
            probs[..., :cache_slots],
            cache_values,
            preferred_element_type=jnp.float32,
        )
        context = context + jnp.einsum(
            "rkgs,rskd->rkgd",
            probs[..., cache_slots:],
            recent_values,
            preferred_element_type=jnp.float32,
        )
        outputs.append(context.reshape(row_count, query_width).astype(jnp.bfloat16))
    return jnp.stack(outputs)


def solution(mesh):
    placed = (
        P(None, "rollout", "tensor"),
        P(None, "tensor"),
        P(None, None, "tensor"),
        P("tensor"),
        P(None, "tensor"),
        P(("rollout", "tensor"), None, None, None),
        P(("rollout", "tensor"), None, None),
        P(None, "rollout", None, "tensor"),
        P("rollout"),
        P(),
    )
    return jax.shard_map(
        body, mesh=mesh, in_specs=placed, out_specs=P(None, "rollout", "tensor"), check_vma=False
    )
```

profile of v0, /device:TPU:1, one launch (start us, length us, event | category | flops | bytes accessed | tf_op | source)
XLA Modules:
  0.0 321.0 jit_solution(1598020490035831530)
XLA Ops:
  7.4 1.0 slice_bitcast_fusion.9
  8.4 1.9 slice_bitcast_fusion.3
  10.2 2.1 slice_bitcast_fusion.2
  12.3 0.7 fusion.160
  14.9 2.4 maximum_select_fusion
  17.3 1.8 maximum_select_fusion.1
  19.3 1.0 fusion.155
  20.3 0.5 all-gather.13.cloned.1.call-update
  20.9 0.5 all-gather.15.cloned.1.call-update
  21.5 0.7 all-gather.11.cloned.1.call-update
  22.3 10.2 %fusion.154 = (bf16[8192,1,128]{2,1,0:T(2,128)(2,1)}, bf16[8192,1,128]{2,1,0:T(2,128)(2,1)}) fusion(bf16[8192,2,128]{2,1,0:T(2,128)(2,1)} %param.12), kind=kLoop, calls=%fused_computation.214 | loop fusion | bytes 8388608 | tf_op jit(solution)/shard_map/slice | solution.py:56
  32.5 8.4 %copy.122 = bf16[8192,1,128]{0,2,1:T(8,128)(2,1)S(1)} copy(bf16[8192,1,128]{2,1,0:T(2,128)(2,1)} %get-tuple-element.13) | data formatting | bytes 4194304
  40.9 9.3 %copy.121 = bf16[8192,1,128]{0,2,1:T(8,128)(2,1)} copy(bf16[8192,1,128]{2,1,0:T(2,128)(2,1)} %get-tuple-element.12) | data formatting | bytes 4194304
  50.2 12.1 %copy.82 = bf16[8192,512]{0,1:T(8,128)(2,1)} copy(bf16[8192,512]{1,0:T(8,128)(2,1)} %param.11) | data formatting | bytes 16777216 | tf_op args[1]
  62.3 1.8 multiply_cosine_fusion
  64.1 141.7 %all-reduce.3.cloned.1.call-done = (bf16[64,9216]{1,0:T(8,128)(2,1)}, bf16[64,9216]{1,0:T(8,128)(2,1)}, bf16[64,12288]{1,0:T(8,128)(2,1)}) async-done(((bf16[64,9216]{1,0:T(8,128)(2,1)}, bf16[64,9216]{1,0:T(8,128)(2,1)}, bf16[64,12288]{1,0:T(8,128)(2,1)}), (bf16[64,9216]{1,0:T(8,128)(2,1)}, bf16[64,9216]{1,0:T(8,128)(2,1)}, bf16[64,12288]{1,0:T(8,128)(2,1)})) %all-reduce.3.cloned.1.call-update) | async-done | bytes 3932176 | tf_op jit(solution)/shard_map/psum | solution.py:13
  205.8 1.1 slice.253
  206.9 0.9 slice.251
  207.8 1.1 slice.249
  208.9 3.5 %fusion.1 = bf16[8192,128]{0,1:T(8,128)(2,1)} fusion(bf16[8192,1,128]{0,2,1:T(8,128)(2,1)S(1)} %copy.122, bf16[64,9216]{1,0:T(8,128)(2,1)} %get-tuple-element.9, bf16[64,1024]{1,0:T(8,128)(2,1)S(1)} %slice.253, s32[]{:T(128)S(6)} %select_n.51), kind=kOutput, calls=%fused_computation.5 | convolution fusion | flops 137363456 | bytes 5259268 | tf_op jit(solution)/shard_map/dot_general | solution.py:73
  212.3 3.8 %fusion = bf16[8192,128]{0,1:T(8,128)(2,1)} fusion(bf16[8192,1,128]{0,2,1:T(8,128)(2,1)S(1)} %copy-done.1, bf16[64,9216]{1,0:T(8,128)(2,1)} %get-tuple-element.10, bf16[64,1024]{1,0:T(8,128)(2,1)S(1)} %slice.251, s32[]{:T(128)S(6)} %select_n.51), kind=kOutput, calls=%fused_computation.4 | convolution fusion | flops 137363456 | bytes 5259268 | tf_op jit(solution)/shard_map/dot_general | solution.py:73
  216.1 5.7 %add_convert_fusion = bf16[8192,512]{0,1:T(8,128)(2,1)} fusion(bf16[8192,512]{0,1:T(8,128)(2,1)S(1)} %copy-done, bf16[64,12288]{1,0:T(8,128)(2,1)S(1)} %copy-done.2, bf16[64,4096]{1,0:T(8,128)(2,1)S(1)} %slice.249, s32[]{:T(128)S(6)} %select_n.48), kind=kOutput, calls=%fused_computation | convolution fusion | flops 549453824 | bytes 17891332 | tf_op jit(solution)/shard_map/dot_general | solution.py:73
  221.9 10.7 %fusion.37 = f32[128,768]{0,1:T(8,128)S(1)} fusion(bf16[1,128,8192]{2,1,0:T(8,128)(2,1)} %all-gather.9.cloned.1.call-done, f32[768]{0:T(1024)S(1)} %pad_maximum_fusion.6, bf16[8192,128]{0,1:T(8,128)(2,1)S(1)} %copy-done.3, bf16[8192,128]{0,1:T(8,128)(2,1)} %fusion, bf16[8192,512]{0,1:T(8,128)(2,1)} %add_convert_fusion), kind=kOutput, calls=%fused_computation.42 | convolution fusion | flops 1648459776 | bytes 15076352 | tf_op jit(solution)/shard_map/dot_general | solution.py:85
  232.7 10.7 %fusion.49 = f32[128,768]{0,1:T(8,128)S(1)} fusion(bf16[1,128,8192]{2,1,0:T(8,128)(2,1)} %all-gather.13.cloned.1.call-done, f32[768]{0:T(1024)S(1)} %pad_maximum_fusion.6, bf16[8192,128]{0,1:T(8,128)(2,1)S(1)} %copy-done.3, bf16[8192,128]{0,1:T(8,128)(2,1)} %fusion, bf16[8192,512]{0,1:T(8,128)(2,1)} %add_convert_fusion), kind=kOutput, calls=%fused_computation.46 | convolution fusion | flops 1648459776 | bytes 15076352 | tf_op jit(solution)/shard_map/dot_general | solution.py:85
  243.5 10.9 %fusion.55 = f32[128,768]{0,1:T(8,128)S(1)} fusion(bf16[1,128,8192]{2,1,0:T(8,128)(2,1)} %all-gather.15.cloned.1.call-done, f32[768]{0:T(1024)} %copy-done.29, bf16[8192,128]{0,1:T(8,128)(2,1)S(1)} %copy-done.3, bf16[8192,128]{0,1:T(8,128)(2,1)} %fusion, bf16[8192,512]{0,1:T(8,128)(2,1)} %add_convert_fusion), kind=kOutput, calls=%fused_computation.48 | convolution fusion | flops 1648459776 | bytes 15076352 | tf_op jit(solution)/shard_map/dot_general | solution.py:85
  254.4 0.7 slice_bitcast_fusion.13
  255.1 0.6 slice_bitcast_fusion.10
  255.7 0.6 slice_bitcast_fusion.11
  256.4 10.9 %fusion.43 = f32[128,768]{0,1:T(8,128)S(1)} fusion(bf16[1,128,8192]{2,1,0:T(8,128)(2,1)} %all-gather.11.cloned.1.call-done, f32[768]{0:T(1024)} %copy-done.29, bf16[8192,128]{0,1:T(8,128)(2,1)S(1)} %copy-done.3, bf16[8192,128]{0,1:T(8,128)(2,1)} %fusion, bf16[8192,512]{0,1:T(8,128)(2,1)} %add_convert_fusion), kind=kOutput, calls=%fused_computation.44 | convolution fusion | flops 1648459776 | bytes 15076352 | tf_op jit(solution)/shard_map/dot_general | solution.py:85
  267.3 0.6 slice_bitcast_fusion.12
  267.9 0.6 fusion.136
  268.9 1.0 subtract_convert_fusion.3
  269.9 0.2 pad_maximum_fusion.2
  270.1 4.4 %fusion.16 = f32[128,4,128]{2,1,0:T(4,128)S(1)} fusion(bf16[128,4,128]{2,1,0:T(4,128)(2,1)S(1)} %pad_maximum_fusion.2, bf16[2,128,128,128]{3,2,1,0:T(8,128)(2,1)} %param.17), kind=kOutput, calls=%fused_computation.20 | convolution fusion | flops 16777216 | bytes 4587520 | tf_op jit(solution)/shard_map/rkgd,rckd->rkgc/dot_general | solution.py:120
  274.5 0.2 copy.87
  275.3 0.2 pad_maximum_fusion.3
  275.4 4.4 %fusion.14 = f32[128,4,128]{2,1,0:T(4,128)S(1)} fusion(bf16[128,4,128]{2,1,0:T(4,128)(2,1)S(1)} %pad_maximum_fusion.3, bf16[2,128,128,128]{3,2,1,0:T(8,128)(2,1)} %param.17), kind=kOutput, calls=%fused_computation.18 | convolution fusion | flops 16777216 | bytes 4587520 | tf_op jit(solution)/shard_map/rkgd,rckd->rkgc/dot_general | solution.py:120
  279.9 0.2 copy.96
  280.3 0.1 copy.127
  280.6 4.5 %fusion.12 = f32[128,4,128]{2,1,0:T(4,128)S(1)} fusion(bf16[2,128,128,128]{3,2,1,0:T(8,128)(2,1)} %param.17, bf16[128,4,64]{2,1,0:T(4,128)(2,1)S(1)} %get-tuple-element.26, bf16[128,4,64]{2,1,0:T(4,128)(2,1)S(1)} %get-tuple-element.25), kind=kOutput, calls=%fused_computation.16 | convolution fusion | flops 17039360 | bytes 4587520 | tf_op jit(solution)/shard_map/rkgd,rckd->rkgc/dot_general | solution.py:120
  285.2 0.2 copy.104
  285.8 4.5 %fusion.10 = f32[128,4,128]{2,1,0:T(4,128)S(1)} fusion(bf16[2,128,128,128]{3,2,1,0:T(8,128)(2,1)} %param.17, bf16[128,4,64]{2,1,0:T(4,128)(2,1)S(1)} %get-tuple-element.24, bf16[128,4,64]{2,1,0:T(4,128)(2,1)S(1)} %get-tuple-element.23), kind=kOutput, calls=%fused_computation.14 | convolution fusion | flops 17039360 | bytes 4587520 | tf_op jit(solution)/shard_map/rkgd,rckd->rkgc/dot_general | solution.py:120
  290.3 0.2 copy.112
  290.5 0.2 fusion.140
  290.8 0.4 fusion.131
  291.4 0.3 fusion.152
  291.9 0.5 fusion.89
  292.4 0.2 fusion.97
  292.9 0.3 fusion.153
  293.4 0.2 fusion.98
  293.9 0.3 fusion.162
  294.3 0.2 fusion.99
  294.8 0.3 fusion.161
  295.3 0.2 fusion.100
  295.7 0.2 copy.116
  296.3 0.3 fusion.165
  296.6 3.4 %fusion.70 = bf16[128,4,128]{2,1,0:T(4,128)(2,1)S(1)} fusion(f32[128,4,128]{2,1,0:T(4,128)S(1)} %fusion.165, bf16[128,4,128]{2,1,0:T(4,128)(2,1)S(1)} %copy.115, bf16[2,128,128,128]{3,2,1,0:T(8,128)(2,1)} %param.17), kind=kOutput, calls=%fused_computation.53 | convolution fusion | flops 16908288 | bytes 4718592 | tf_op jit(solution)/shard_map/rkgc,rckd->rkgd/dot_general | solution.py:134
  300.0 0.2 copy.108
  300.5 0.3 fusion.164
  300.8 3.6 %fusion.73 = bf16[128,4,128]{2,1,0:T(4,128)(2,1)S(1)} fusion(f32[128,4,128]{2,1,0:T(4,128)S(1)} %fusion.164, bf16[128,4,128]{2,1,0:T(4,128)(2,1)S(1)} %copy.107, bf16[2,128,128,128]{3,2,1,0:T(8,128)(2,1)} %param.17), kind=kOutput, calls=%fused_computation.54 | convolution fusion | flops 16908288 | bytes 4718592 | tf_op jit(solution)/shard_map/rkgc,rckd->rkgd/dot_general | solution.py:134
  304.9 0.3 fusion.163
  305.2 3.4 %fusion.76 = bf16[128,4,128]{2,1,0:T(4,128)(2,1)S(1)} fusion(f32[128,4,128]{2,1,0:T(4,128)S(1)} %fusion.163, bf16[128,4,128]{2,1,0:T(4,128)(2,1)S(1)} %copy.99, bf16[2,128,128,128]{3,2,1,0:T(8,128)(2,1)} %param.17), kind=kOutput, calls=%fused_computation.55 | convolution fusion | flops 16908288 | bytes 4718592 | tf_op jit(solution)/shard_map/rkgc,rckd->rkgd/dot_general | solution.py:134
  309.1 3.4 %fusion.79 = bf16[128,4,128]{2,1,0:T(4,128)(2,1)S(1)} fusion(bf16[128,4,128]{2,1,0:T(4,128)(2,1)S(1)} %copy.91, bf16[2,128,128,128]{3,2,1,0:T(8,128)(2,1)} %param.17, f32[128,128]{1,0:T(8,128)S(1)} %copy.93, f32[128,4]{1,0:T(8,128)S(1)} %copy.92), kind=kOutput, calls=%fused_computation.56 | convolution fusion | flops 16973824 | bytes 4524032 | tf_op jit(solution)/shard_map/rkgc,rckd->rkgd/dot_general | solution.py:134
  312.5 0.9 pad_maximum_fusion.1
  (155 shorter events, 5.6 us)
Async XLA Ops:
  7.4 4.9 %copy-start.28 = (s32[3]{0:T(128)S(1)}, s32[3]{0:T(128)}, u32[]{:S(2)}) copy-start(s32[3]{0:T(128)} %param.19) | copy-start | bytes 40
  7.4 198.4 %all-reduce.3.cloned.1.call-start = ((), (), s32[]{:S(2)}) async-start(), calls=%async_computation.4 | async-start | bytes 7864320 | tf_op jit(solution)/shard_map/psum | solution.py:13
  17.3 1.9 copy-start.4
  19.2 3.0 copy-start.31
  19.2 3.1 copy-start.32
  19.2 202.7 %all-gather.9.cloned.1.call-start = ((), (), s32[]{:S(2)}) async-start(), calls=%async_computation | async-start | bytes 2359296 | tf_op jit(solution)/shard_map/all_gather | solution.py:88
  20.3 212.4 %all-gather.13.cloned.1.call-start = ((), (), s32[]{:S(2)}) async-start(), calls=%async_computation.2 | async-start | bytes 2359296 | tf_op jit(solution)/shard_map/all_gather | solution.py:88
  20.9 222.6 %all-gather.15.cloned.1.call-start = ((), (), s32[]{:S(2)}) async-start(), calls=%async_computation.3 | async-start | bytes 2359296 | tf_op jit(solution)/shard_map/all_gather | solution.py:88
  21.5 234.9 %all-gather.11.cloned.1.call-start = ((), (), s32[]{:S(2)}) async-start(), calls=%async_computation.1 | async-start | bytes 2359296 | tf_op jit(solution)/shard_map/all_gather | solution.py:88
  22.2 40.0 %copy-start.18 = (f32[64]{0:T(128)}, f32[64]{0:T(128)S(1)}, u32[]{:S(2)}) copy-start(f32[64]{0:T(128)S(1)} %multiply_exponential_fusion) | copy-start | bytes 772
  22.2 40.0 %copy-start.20 = (f32[128]{0:T(128)}, f32[128]{0:T(128)S(1)}, u32[]{:S(2)}) copy-start(f32[128]{0:T(128)S(1)} %get-tuple-element.81) | copy-start | bytes 1540
  22.3 40.0 %copy-start.22 = (f32[128]{0:T(128)}, f32[128]{0:T(128)S(1)}, u32[]{:S(2)}) copy-start(f32[128]{0:T(128)S(1)} %get-tuple-element.83) | copy-start | bytes 1540
  22.3 40.0 %copy-start.24 = (f32[128]{0:T(128)}, f32[128]{0:T(128)S(1)}, u32[]{:S(2)}) copy-start(f32[128]{0:T(128)S(1)} %get-tuple-element.84) | copy-start | bytes 1540
  22.3 40.0 %copy-start.26 = (f32[128]{0:T(128)}, f32[128]{0:T(128)S(1)}, u32[]{:S(2)}) copy-start(f32[128]{0:T(128)S(1)} %get-tuple-element.82) | copy-start | bytes 1540
  50.2 12.1 %copy-start.30 = (f32[512]{0:T(512)S(1)}, f32[512]{0:T(512)}, u32[]{:S(2)}) copy-start(f32[512]{0:T(512)} %param.13) | copy-start | bytes 6148
  62.2 170.4 %copy-start.29 = (f32[768]{0:T(1024)}, f32[768]{0:T(1024)S(1)}, u32[]{:S(2)}) copy-start(f32[768]{0:T(1024)S(1)} %pad_maximum_fusion.6) | copy-start | bytes 9220
  205.8 6.5 %copy-start.1 = (bf16[8192,1,128]{0,2,1:T(8,128)(2,1)S(1)}, bf16[8192,1,128]{0,2,1:T(8,128)(2,1)}, u32[]{:S(2)}) copy-start(bf16[8192,1,128]{0,2,1:T(8,128)(2,1)} %copy.121) | copy-start | bytes 6291460
  208.9 7.3 %copy-start = (bf16[8192,512]{0,1:T(8,128)(2,1)S(1)}, bf16[8192,512]{0,1:T(8,128)(2,1)}, u32[]{:S(2)}) copy-start(bf16[8192,512]{0,1:T(8,128)(2,1)} %copy.82) | copy-start | bytes 25165828
  208.9 7.2 %copy-start.2 = (bf16[64,12288]{1,0:T(8,128)(2,1)S(1)}, bf16[64,12288]{1,0:T(8,128)(2,1)}, u32[]{:S(2)}) copy-start(bf16[64,12288]{1,0:T(8,128)(2,1)} %get-tuple-element.11) | copy-start | bytes 4718596
  216.1 5.8 %copy-start.3 = (bf16[8192,128]{0,1:T(8,128)(2,1)S(1)}, bf16[8192,128]{0,1:T(8,128)(2,1)}, u32[]{:S(2)}) copy-start(bf16[8192,128]{0,1:T(8,128)(2,1)} %fusion.1) | copy-start | bytes 6291460
  243.4 25.1 %copy-start.6 = (f32[128,768]{0,1:T(8,128)}, f32[128,768]{0,1:T(8,128)S(1)}, u32[]{:S(2)}) copy-start(f32[128,768]{0,1:T(8,128)S(1)} %fusion.49) | copy-start | bytes 1179652
  254.4 13.5 %copy-start.5 = (f32[128,768]{0,1:T(8,128)}, f32[128,768]{0,1:T(8,128)S(1)}, u32[]{:S(2)}) copy-start(f32[128,768]{0,1:T(8,128)S(1)} %fusion.55) | copy-start | bytes 1179652
  268.6 6.5 %copy-start.11 = (f32[128,64]{1,0:T(8,128)S(1)}, f32[128,64]{1,0:T(8,128)}, u32[]{:S(2)}) copy-start(f32[128,64]{1,0:T(8,128)} %get-tuple-element.75) | copy-start | bytes 98308
  268.6 6.5 %copy-start.12 = (f32[128,64]{1,0:T(8,128)S(1)}, f32[128,64]{1,0:T(8,128)}, u32[]{:S(2)}) copy-start(f32[128,64]{1,0:T(8,128)} %get-tuple-element.76) | copy-start | bytes 98308
  274.5 5.5 %slice-start.1 = ((f32[128,768]{0,1:T(8,128)}), f32[128,512]{0,1:T(8,128)S(1)}, s32[]{:S(2)}) async-start(f32[128,768]{0,1:T(8,128)} %copy-done.6), calls=%async_computation.6 | async-start | bytes 524288 | tf_op jit(solution)/shard_map/slice | solution.py:103
  274.8 5.7 %copy-start.9 = (f32[128,64]{1,0:T(8,128)S(1)}, f32[128,64]{1,0:T(8,128)}, u32[]{:S(2)}) copy-start(f32[128,64]{1,0:T(8,128)} %get-tuple-element.77) | copy-start | bytes 98308
  274.8 5.7 %copy-start.10 = (f32[128,64]{1,0:T(8,128)S(1)}, f32[128,64]{1,0:T(8,128)}, u32[]{:S(2)}) copy-start(f32[128,64]{1,0:T(8,128)} %get-tuple-element.78) | copy-start | bytes 98308
  279.9 5.5 %slice-start = ((f32[128,768]{0,1:T(8,128)}), f32[128,512]{0,1:T(8,128)S(1)}, s32[]{:S(2)}) async-start(f32[128,768]{0,1:T(8,128)} %copy-done.5), calls=%async_computation.5 | async-start | bytes 524288 | tf_op jit(solution)/shard_map/slice | solution.py:103
  280.1 5.6 %copy-start.7 = (f32[128,64]{1,0:T(8,128)S(1)}, f32[128,64]{1,0:T(8,128)}, u32[]{:S(2)}) copy-start(f32[128,64]{1,0:T(8,128)} %get-tuple-element.61) | copy-start | bytes 98308
  280.1 5.6 %copy-start.8 = (f32[128,64]{1,0:T(8,128)S(1)}, f32[128,64]{1,0:T(8,128)}, u32[]{:S(2)}) copy-start(f32[128,64]{1,0:T(8,128)} %get-tuple-element.62) | copy-start | bytes 98308
  285.1 5.4 %copy-start.13 = (f32[128,1,128]{0,2,1:T(8,128)S(1)}, f32[128,1,128]{0,2,1:T(8,128)}, u32[]{:S(2)}) copy-start(f32[128,1,128]{0,2,1:T(8,128)} %slice_bitcast_fusion.12) | copy-start | bytes 196612
  285.1 5.4 %copy-start.19 = (f32[64]{0:T(128)S(1)}, f32[64]{0:T(128)}, u32[]{:S(2)}) copy-start(f32[64]{0:T(128)} %copy-done.18) | copy-start | bytes 772
  285.1 5.4 %copy-start.27 = (f32[128]{0:T(128)S(1)}, f32[128]{0:T(128)}, u32[]{:S(2)}) copy-start(f32[128]{0:T(128)} %copy-done.26) | copy-start | bytes 1540
  285.1 5.7 %copy-start.14 = (f32[128,1,128]{0,2,1:T(8,128)S(1)}, f32[128,1,128]{0,2,1:T(8,128)}, u32[]{:S(2)}) copy-start(f32[128,1,128]{0,2,1:T(8,128)} %slice_bitcast_fusion.13) | copy-start | bytes 196612
  285.1 5.6 %copy-start.15 = (f32[128,1,128]{0,2,1:T(8,128)S(1)}, f32[128,1,128]{0,2,1:T(8,128)}, u32[]{:S(2)}) copy-start(f32[128,1,128]{0,2,1:T(8,128)} %slice_bitcast_fusion.10) | copy-start | bytes 196612
  285.1 5.6 %copy-start.16 = (f32[128,1,128]{0,2,1:T(8,128)S(1)}, f32[128,1,128]{0,2,1:T(8,128)}, u32[]{:S(2)}) copy-start(f32[128,1,128]{0,2,1:T(8,128)} %slice_bitcast_fusion.11) | copy-start | bytes 196612
  285.1 5.6 %copy-start.21 = (f32[128]{0:T(128)S(1)}, f32[128]{0:T(128)}, u32[]{:S(2)}) copy-start(f32[128]{0:T(128)} %copy-done.20) | copy-start | bytes 1540
  285.1 5.6 %copy-start.23 = (f32[128]{0:T(128)S(1)}, f32[128]{0:T(128)}, u32[]{:S(2)}) copy-start(f32[128]{0:T(128)} %copy-done.22) | copy-start | bytes 1540
  285.2 5.6 %copy-start.25 = (f32[128]{0:T(128)S(1)}, f32[128]{0:T(128)}, u32[]{:S(2)}) copy-start(f32[128]{0:T(128)} %copy-done.24) | copy-start | bytes 1540
  292.4 3.6 %copy-start.17 = (bf16[128,1,1,128]{0,3,2,1:T(8,128)(2,1)S(1)}, bf16[128,1,1,128]{0,3,2,1:T(8,128)(2,1)}, u32[]{:S(2)}) copy-start(bf16[128,1,1,128]{0,3,2,1:T(8,128)(2,1)} %fusion.136) | copy-start | bytes 98308
Sparse Core Ops, SparseCore 0:
  19.3 186.4 all-reduce.2
Sparse Core Ops, SparseCore 1:
  22.0 57.1 all-gather.8
  81.3 51.9 all-gather.12
  135.5 52.5 all-gather.14
  190.4 52.7 all-gather.10
where the time goes:
time: 322 us; the launch traced here: 321 us
  waiting for transfers between devices  144 us (45%)
  matrix products  89.9 us (28%)
  local copies, waits for them, and re-layouts  58.1 us (18%)
  between operations  18.1 us (6%)
  other arithmetic  11.2 us (3%)
    psum x1, waiting for transfers between devices, spread(): return lax.psum(jnp.where(mine, shard, jnp.zeros_like(shard)), axis)  142 us
    dot_general x4, matrix products, project(): return jnp.dot(received, merged, preferred_element_type=jnp.float32)  43.3 us
    unnamed x78, local copies, waits for them, and re-layouts  31.2 us
    dot_general x4, matrix products, body(): jnp.einsum('rkgd,rckd->rkgc', grouped, cache_keys, preferred_element_type...  17.8 us
    dot_general x4, matrix products, body(): jnp.einsum('rkgc,rckd->rkgd', probs[..., :cache_slots], cache_values, pre...  13.7 us
    dot_general x3, matrix products, body(): lax.dot_general(down_part, up_part, (((0,), (0,)), ((), ())), preferred_e...  13 us
    slice x1, local copies, waits for them, and re-layouts, body(): base_parts = [w_query, w_keyval[:, 0], w_keyval[:, 1]]  10.2 us
  transfers between devices with their start and end apart: 5, of which 1 were waited for; matrix products, arithmetic and copies ran while one was open for 29% of the time, Pallas kernels for 0%

commit v1 on v0

v1 whole, which is shorter than its diff:
```python
import functools
import math

import jax
import jax.numpy as jnp
from jax import lax
from jax.experimental import pallas as pl
from jax.experimental.pallas import tpu as pltpu
from jax.sharding import PartitionSpec as P

MESH = pl.DeviceIdType.MESH
HD = 128
STEPS = 4
ROWS = 128
TOK = STEPS * ROWS
D = 8192
PART = 1024
RANK = 64
HALF = RANK // 2
QW = 512
KW = 128
QFULL = 4096
KFULL = 1024
NSEM = 80
CROSS = (512, 640)
BF = jnp.bfloat16
F32 = jnp.float32


def coordinates():
    rollout = lax.axis_index("rollout")
    tensor = lax.axis_index("tensor")
    core = rollout % 2
    x = (tensor // 4) * 2 + (rollout // 2) % 2
    return core, x, rollout // 4, tensor % 4


def device(core, x, y, z):
    return ((y * 2 + x % 2) * 2 + core, (x // 2) * 4 + z)


def gather_merge_project(
    owners_ref,
    x_hbm,
    wq_hbm,
    wkv_hbm,
    down_hbm,
    up_hbm,
    bq_ref,
    bkv_ref,
    len_ref,
    q_ref,
    k_ref,
    v_ref,
    xs,
    wq,
    wkv,
    mkv,
    pay,
    rcore,
    ry,
    yq,
    rz,
    rx,
    fac,
    acc,
    cos_ref,
    sin_ref,
    send,
    recv,
    local,
):
    core, x, y, z = coordinates()
    tensor = (x // 2) * 4 + z
    me = ((y * 2 + x % 2) * 2 + core) * 8 + tensor

    def at(dc=0, dx=0, dy=0, dz=0):
        return device((core + dc) % 2, (x + dx) % 4, (y + dy) % 4, (z + dz) % 4)

    z_up, z_down, z_far = at(dz=1), at(dz=3), at(dz=2)
    x_far = at(dx=2)
    y_up, y_down = at(dy=1), at(dy=3)
    other = at(dc=1)
    partners = [z_up, z_down, z_far, at(dx=1), x_far, at(dx=3), y_up, y_down, other]

    locals_used = [0]

    def fetch(src, dst):
        copy = pltpu.make_async_copy(src, dst, local.at[locals_used[0]])
        locals_used[0] += 1
        copy.start()
        return copy

    ups = []
    for t in range(8):
        ups.append(fetch(up_hbm.at[0, :, pl.ds(t * QW, QW)], pay.at[0, :, pl.ds(t * PART, QW)]))
        for j in range(2):
            ups.append(
                fetch(
                    up_hbm.at[0, :, pl.ds(QFULL + j * KFULL + t * KW, KW)],
                    pay.at[0, :, pl.ds(t * PART + QW + j * KW, KW)],
                )
            )
    downs = [fetch(down_hbm.at[0, m], pay.at[1 + m]) for m in range(3)]

    barrier = pltpu.get_barrier_semaphore()
    for partner in partners:
        pl.semaphore_signal(barrier, inc=1, device_id=partner, device_id_type=MESH)
    pl.semaphore_wait(barrier, len(partners))

    used = [0]

    def put(src, dst, target):
        index = used[0]
        used[0] += 1
        copy = pltpu.make_async_remote_copy(
            src_ref=src,
            dst_ref=dst,
            send_sem=send.at[index],
            recv_sem=recv.at[index],
            device_id=target,
            device_id_type=MESH,
        )
        copy.start()
        return copy

    started = []

    def push(src, target, dst=None):
        copy = put(src, src if dst is None else dst, target)
        started.append(copy)
        return copy

    def chunk(t, h, columns=None):
        if columns is None:
            return xs.at[t, pl.ds(2 * h, 2)]
        return xs.at[t, pl.ds(2 * h, 2), :, pl.ds(columns[0], columns[1] - columns[0])]

    def own(h):
        return x_hbm.at[pl.ds(2 * h, 2)]

    base = (x // 2) * 4
    far_base = 4 - base
    z_prev, z_next, z_opp = (z + 3) % 4, (z + 1) % 4, (z + 2) % 4

    to_up, to_down, to_x = [], [], []
    for h in range(2):
        to_up.append(push(own(h), z_up, chunk(tensor, h)))
        to_down.append(push(own(h), z_down, chunk(tensor, h)))
        to_x.append(push(own(h), x_far, chunk(tensor, h)))
    x_load = fetch(x_hbm, xs.at[tensor])
    wq_load = fetch(wq_hbm, wq)
    wkv_load = fetch(wkv_hbm, wkv)

    lane = lax.broadcasted_iota(jnp.int32, (ROWS, HD), 1)
    frequency = jnp.exp(
        -((lane % (HD // 2)).astype(F32) * (2.0 / HD)) * math.log(1000000.0)
    )
    lengths = jnp.broadcast_to(len_ref[...], (ROWS, HD)).astype(F32).T
    sign = jnp.where(lane < HD // 2, -1.0, 1.0)
    for s in range(STEPS):
        angles = (lengths + float(s)) * frequency
        cos_ref[pl.ds(s * ROWS, ROWS), :] = jnp.cos(angles)
        sin_ref[pl.ds(s * ROWS, ROWS), :] = jnp.sin(angles) * sign

    keep = [(owners_ref[m] == me).astype(F32).astype(BF) for m in range(3)]
    for t in range(8):
        pay[0, :, pl.ds(t * PART + QW + 2 * KW, PART - QW - 2 * KW)] = jnp.zeros(
            (RANK, PART - QW - 2 * KW), BF
        )
    for copy in ups:
        copy.wait()

    def mask_up(t, carry):
        start = pl.multiple_of(t * PART, PART)
        spans = [(0, QW), (QW, KW), (QW + KW, KW)]
        for m, (offset, width) in enumerate(spans):
            columns = pl.ds(start + offset, width)
            pay[0, :, columns] = pay[0, :, columns] * keep[m]
        return carry

    lax.fori_loop(0, 8, mask_up, 0)
    for copy in downs:
        copy.wait()

    def mask_down(m):
        def mask_block(t, carry):
            columns = pl.ds(pl.multiple_of(t * PART, PART), PART)
            pay[1 + m, :, columns] = pay[1 + m, :, columns] * keep[m]
            return carry

        lax.fori_loop(0, 8, mask_block, 0)

    mine = pl.multiple_of(core * HALF, HALF)
    theirs = pl.multiple_of((1 - core) * HALF, HALF)
    rows = pl.ds(mine, HALF)

    def core_send(g):
        return push(pay.at[pl.ds(2 * g, 2), pl.ds(theirs, HALF)], other, rcore.at[pl.ds(2 * g, 2)])

    mask_down(0)
    core_copies = [core_send(0)]
    mask_down(1)
    mask_down(2)
    core_copies.append(core_send(1))

    def quarter(q):
        return pl.ds(pl.multiple_of(q * 2048, 2048), 2048)

    def core_sum(g):
        core_copies[g].wait_recv()

        def add_block(t, carry):
            columns = pl.ds(pl.multiple_of(t * PART, PART), PART)
            for m in (2 * g, 2 * g + 1):
                rcore[m, :, columns] = rcore[m, :, columns] + pay[m, rows, columns]
            return carry

        lax.fori_loop(0, 8, add_block, 0)

    y_opp, y_next, y_prev = (y + 2) % 4, (y + 1) % 4, (y + 3) % 4

    def y_first(g):
        a, b = 2 * g, 2 * g + 1
        first = [
            push(rcore.at[a, :, quarter(y_opp)], y_up, ry.at[g, 0]),
            push(rcore.at[b, :, quarter(y_opp)], y_down, ry.at[g, 1]),
        ]
        raw = [
            push(rcore.at[a, :, quarter(y_prev)], y_down, ry.at[g, 2]),
            push(rcore.at[b, :, quarter(y_next)], y_up, ry.at[g, 3]),
        ]
        return first, raw

    def y_second(g, first):
        a, b = 2 * g, 2 * g + 1
        first[0].wait_recv()
        ry[g, 0] = ry[g, 0] + rcore[a, :, quarter(y_next)]
        up = push(ry.at[g, 0], y_up, ry.at[g, 4])
        first[1].wait_recv()
        ry[g, 1] = ry[g, 1] + rcore[b, :, quarter(y_prev)]
        down = push(ry.at[g, 1], y_down, ry.at[g, 5])
        return up, down

    def y_third(g, raw, combined):
        a, b = 2 * g, 2 * g + 1
        for copy in (*raw, *combined):
            copy.wait_recv()
        yq[a] = rcore[a, :, quarter(y)] + ry[g, 2] + ry[g, 4]
        yq[b] = rcore[b, :, quarter(y)] + ry[g, 3] + ry[g, 5]

    def part_z(zz):
        return pl.ds(pl.multiple_of(zz * 512, 512), 512)

    def span_z(zz):
        return pl.ds(pl.multiple_of(y * 2048 + zz * 512, 512), 512)

    def span_x(xx):
        return pl.ds(pl.multiple_of(y * 2048 + z * 512 + xx * 128, 128), 128)

    def members(g):
        return pl.ds(2 * g, 2)

    def z_reduce_start(g):
        return [
            push(yq.at[members(g), :, part_z((z + d) % 4)], at(dz=d), rz.at[g, d - 1])
            for d in (1, 2, 3)
        ]

    def z_reduce_end(g, copies):
        for copy in copies:
            copy.wait_recv()
        total = yq[members(g), :, part_z(z)]
        for d in range(3):
            total = total + rz[g, d]
        rz[g, 3] = total

    def x_reduce_start(g):
        return [
            push(
                rz.at[g, 3, :, :, pl.ds(pl.multiple_of(((x + d) % 4) * 128, 128), 128)],
                at(dx=d),
                rx.at[g, d - 1],
            )
            for d in (1, 2, 3)
        ]

    def x_reduce_end(g, copies):
        for copy in copies:
            copy.wait_recv()
        total = rz[g, 3, :, :, pl.ds(pl.multiple_of(x * 128, 128), 128)]
        for d in range(3):
            total = total + rx[g, d]
        rx[g, 3] = total

    def x_spread_start(g):
        return [
            push(rx.at[g, 3], at(dx=d), fac.at[members(g), rows, span_x(x)])
            for d in (1, 2, 3)
        ]

    def x_spread_end(g, copies):
        fac[members(g), rows, span_x(x)] = rx[g, 3]
        for copy in copies:
            copy.wait_recv()

    def z_spread_start(g):
        piece = fac.at[members(g), rows, span_z(z)]
        return [push(piece, at(dz=d)) for d in (1, 2, 3)]

    def wait_all(copies):
        for copy in copies:
            copy.wait_recv()

    def y_spread_start(g):
        piece = fac.at[members(g), rows, quarter(y)]
        return [push(piece, y_up), push(piece, y_down), push(piece, other)]

    def y_forward(g, copies):
        copies[0].wait_recv()
        up = push(fac.at[2 * g, rows, quarter(y_prev)], y_up)
        down_core = push(fac.at[members(g), rows, quarter(y_prev)], other)
        copies[1].wait_recv()
        down = push(fac.at[2 * g + 1, rows, quarter(y_next)], y_down)
        up_core = push(fac.at[members(g), rows, quarter(y_next)], other)
        return up, down, down_core, up_core

    def y_last(g, forwards):
        forwards[0].wait_recv()
        forwards[1].wait_recv()
        return push(fac.at[members(g), rows, quarter(y_opp)], other)

    core_sum(0)
    first0, raw0 = y_first(0)
    core_sum(1)
    first1, raw1 = y_first(1)
    comb0 = y_second(0, first0)

    far_slot = far_base + z
    fwd = {}
    to_up[0].wait_recv()
    fwd["z0"] = push(chunk(base + z_prev, 0), z_up)
    fwd["b_prev0"] = push(chunk(base + z_prev, 0, (CROSS[0], PART)), x_far)
    to_down[0].wait_recv()
    fwd["b_next0"] = push(chunk(base + z_next, 0, (CROSS[0], PART)), x_far)
    to_x[0].wait_recv()
    fwd["a_up0"] = push(chunk(far_slot, 0, (0, CROSS[0])), z_up)
    fwd["a_down0"] = push(chunk(far_slot, 0, (0, CROSS[0])), z_down)

    comb1 = y_second(1, first1)
    y_third(0, raw0, comb0)
    zr0 = z_reduce_start(0)
    z_reduce_end(0, zr0)
    xr0 = x_reduce_start(0)
    y_third(1, raw1, comb1)
    zr1 = z_reduce_start(1)
    x_reduce_end(0, xr0)
    xs0 = x_spread_start(0)
    z_reduce_end(1, zr1)
    xr1 = x_reduce_start(1)
    x_spread_end(0, xs0)
    zs0 = z_spread_start(0)

    to_down[1].wait_recv()
    fwd["z1"] = push(chunk(base + z_next, 1), z_down)
    fwd["b_next1"] = push(chunk(base + z_next, 1, (CROSS[1], PART)), x_far)
    to_up[1].wait_recv()
    fwd["b_prev1"] = push(chunk(base + z_prev, 1, (CROSS[1], PART)), x_far)
    to_x[1].wait_recv()
    fwd["a_up1"] = push(chunk(far_slot, 1, (0, CROSS[1])), z_up)
    fwd["a_down1"] = push(chunk(far_slot, 1, (0, CROSS[1])), z_down)

    x_reduce_end(1, xr1)
    xs1 = x_spread_start(1)
    wait_all(zs0)
    ys0 = y_spread_start(0)
    x_spread_end(1, xs1)
    zs1 = z_spread_start(1)
    wait_all(zs1)
    ys1 = y_spread_start(1)

    fwd["z0"].wait_recv()
    fwd["b_opp0"] = push(chunk(base + z_opp, 0, (CROSS[0], PART)), x_far)
    fwd["z1"].wait_recv()
    fwd["b_opp1"] = push(chunk(base + z_opp, 1, (CROSS[1], PART)), x_far)
    yf0 = y_forward(0, ys0)
    yf1 = y_forward(1, ys1)
    fwd["a_up0"].wait_recv()
    fwd["a_opp0"] = push(chunk(far_base + z_prev, 0, (0, CROSS[0])), z_up)
    fwd["a_down1"].wait_recv()
    fwd["a_opp1"] = push(chunk(far_base + z_next, 1, (0, CROSS[1])), z_down)
    core0 = y_last(0, yf0)
    core1 = y_last(1, yf1)
    for copy in (ys0[2], ys1[2], yf0[2], yf0[3], yf1[2], yf1[3], core0, core1):
        copy.wait_recv()
    for name in ("a_down0", "a_up1", "a_opp0", "a_opp1"):
        fwd[name].wait_recv()
    for name in ("b_prev0", "b_next0", "b_prev1", "b_next1", "b_opp0", "b_opp1"):
        fwd[name].wait_recv()
    for copy in started:
        copy.wait_send()

    x_load.wait()
    wq_load.wait()
    wkv_load.wait()
    up_columns = pl.multiple_of(tensor * PART, PART)
    block = 512

    def merge(i, carry):
        ks = pl.ds(pl.multiple_of(i * block, block), block)
        low = lax.dot_general(
            fac[1, :, ks],
            fac[0, :, pl.ds(up_columns, QW)],
            (((0,), (0,)), ((), ())),
            preferred_element_type=F32,
        )
        wq[ks, :] = (wq[ks, :].astype(F32) + low).astype(BF)
        for j in range(2):
            low = lax.dot_general(
                fac[2 + j, :, ks],
                fac[0, :, pl.ds(up_columns + QW + j * KW, KW)],
                (((0,), (0,)), ((), ())),
                preferred_element_type=F32,
            )
            mkv[ks, pl.ds(j * KW, KW)] = (wkv[ks, pl.ds(j * KW, KW)].astype(F32) + low).astype(BF)
        return carry

    lax.fori_loop(0, D // block, merge, 0)
    acc[...] = jnp.zeros_like(acc)

    def project(t, carry):
        ks = pl.ds(pl.multiple_of(t * PART, PART), PART)
        received = xs[t].reshape(TOK, PART)
        acc[:, pl.ds(0, QW)] += jnp.dot(received, wq[ks, :], preferred_element_type=F32)
        acc[:, pl.ds(QW, 2 * KW)] += jnp.dot(received, mkv[ks, :], preferred_element_type=F32)
        return carry

    lax.fori_loop(0, 8, project, 0)

    def rotate(vectors, token_rows):
        return vectors * cos_ref[token_rows, :] + pltpu.roll(vectors, HD // 2, 1) * sin_ref[token_rows, :]

    for s in range(STEPS):
        token_rows = pl.ds(s * ROWS, ROWS)
        for h in range(QW // HD):
            columns = pl.ds(h * HD, HD)
            turned = rotate(acc[token_rows, columns] + bq_ref[:, columns], token_rows)
            q_ref[:, s * 4 + h, :] = turned.astype(BF).astype(F32)
        turned = rotate(acc[token_rows, pl.ds(QW, KW)] + bkv_ref[pl.ds(0, 1), :], token_rows)
        k_ref[s] = turned.astype(BF)
        v_ref[s] = (acc[token_rows, pl.ds(QW + KW, KW)] + bkv_ref[pl.ds(1, 1), :]).astype(BF)


BLOCK = 32


def attend(len_ref, q_ref, k_ref, v_ref, cache_ref, o_ref, recent, recent_probs, context):
    first = pl.program_id(0) * BLOCK
    queries = q_ref[...].reshape(BLOCK * 16, HD).astype(BF)
    keys = k_ref[...].reshape(BLOCK * STEPS, HD)
    scale = 1.0 / math.sqrt(HD)
    scores = (
        lax.dot_general(queries, keys, (((1,), (1,)), ((), ())), preferred_element_type=F32) * scale
    )
    row = lax.broadcasted_iota(jnp.int32, scores.shape, 0)
    lane = lax.broadcasted_iota(jnp.int32, scores.shape, 1)
    valid = (row // 16 == lane % BLOCK) & (lane // BLOCK <= (row // 4) % 4)
    recent[...] = jnp.where(valid, scores, -1e30)
    slots = lax.broadcasted_iota(jnp.int32, (16, HD), 1)

    def one_row(r):
        mine = pl.ds(r * 16, 16)
        q = q_ref[r].astype(BF)
        cached = (
            lax.dot_general(q, cache_ref[0, r], (((1,), (1,)), ((), ())), preferred_element_type=F32)
            * scale
        )
        cached = jnp.where(slots < len_ref[first + r], cached, -1e30)
        fresh = recent[mine, :]
        top = jnp.max(jnp.maximum(cached, fresh), axis=1, keepdims=True)
        cached = jnp.exp(cached - top)
        fresh = jnp.exp(fresh - top)
        total = jnp.sum(cached + fresh, axis=1, keepdims=True)
        recent_probs[mine, :] = (fresh / total).astype(BF)
        context[r] = jnp.dot((cached / total).astype(BF), cache_ref[1, r], preferred_element_type=F32)

    for r in range(BLOCK):
        one_row(r)
    values = v_ref[...].reshape(BLOCK * STEPS, HD)
    context[...] += jnp.dot(recent_probs[...], values, preferred_element_type=F32).reshape(
        BLOCK, 16, HD
    )
    for s in range(STEPS):
        for h in range(4):
            o_ref[s, :, pl.ds(h * HD, HD)] = context[:, s * 4 + h, :].astype(BF)


def body(
    inputs,
    w_query,
    w_keyval,
    bias_query,
    bias_keyval,
    factor_down,
    factor_up,
    cache,
    lengths,
    owners,
):
    any_space = pl.BlockSpec(memory_space=pl.ANY)
    vmem = pl.BlockSpec(memory_space=pltpu.VMEM)
    smem = pl.BlockSpec(memory_space=pltpu.SMEM)
    queries, keys, values = pl.pallas_call(
        gather_merge_project,
        out_shape=(
            jax.ShapeDtypeStruct((ROWS, 16, HD), F32),
            jax.ShapeDtypeStruct((STEPS, ROWS, HD), BF),
            jax.ShapeDtypeStruct((STEPS, ROWS, HD), BF),
        ),
        in_specs=[smem] + [any_space] * 5 + [vmem] * 3,
        out_specs=(vmem, vmem, vmem),
        scratch_shapes=[
            pltpu.VMEM((8, STEPS, ROWS, PART), BF),
            pltpu.VMEM((D, QW), BF),
            pltpu.VMEM((D, 2 * KW), BF),
            pltpu.VMEM((D, 2 * KW), BF),
            pltpu.VMEM((4, RANK, D), BF),
            pltpu.VMEM((4, HALF, D), BF),
            pltpu.VMEM((2, 6, HALF, 2048), BF),
            pltpu.VMEM((4, HALF, 2048), BF),
            pltpu.VMEM((2, 4, 2, HALF, 512), BF),
            pltpu.VMEM((2, 4, 2, HALF, 128), BF),
            pltpu.VMEM((4, RANK, D), BF),
            pltpu.VMEM((TOK, QW + 2 * KW), F32),
            pltpu.VMEM((TOK, HD), F32),
            pltpu.VMEM((TOK, HD), F32),
            pltpu.SemaphoreType.DMA((NSEM,)),
            pltpu.SemaphoreType.DMA((NSEM,)),
            pltpu.SemaphoreType.DMA((32,)),
        ],
        compiler_params=pltpu.CompilerParams(
            collective_id=0, has_side_effects=True, vmem_limit_bytes=56 << 20
        ),
    )(
        owners,
        inputs,
        w_query,
        w_keyval.reshape(D, 2 * KW),
        factor_down,
        factor_up,
        bias_query.reshape(1, QW),
        bias_keyval,
        lengths.reshape(1, ROWS),
    )
    return pl.pallas_call(
        attend,
        grid=(ROWS // BLOCK,),
        out_shape=jax.ShapeDtypeStruct((STEPS, ROWS, QW), BF),
        in_specs=[
            smem,
            pl.BlockSpec((BLOCK, 16, HD), lambda i: (i, 0, 0)),
            pl.BlockSpec((STEPS, BLOCK, HD), lambda i: (0, i, 0)),
            pl.BlockSpec((STEPS, BLOCK, HD), lambda i: (0, i, 0)),
            pl.BlockSpec((2, BLOCK, HD, HD), lambda i: (0, i, 0, 0)),
        ],
        out_specs=pl.BlockSpec((STEPS, BLOCK, QW), lambda i: (0, i, 0)),
        scratch_shapes=[
            pltpu.VMEM((BLOCK * 16, HD), F32),
            pltpu.VMEM((BLOCK * 16, HD), BF),
            pltpu.VMEM((BLOCK, 16, HD), F32),
        ],
        compiler_params=pltpu.CompilerParams(vmem_limit_bytes=32 << 20),
    )(lengths, queries, keys, values, cache)


def solution(mesh):
    placed = (
        P(None, "rollout", "tensor"),
        P(None, "tensor"),
        P(None, None, "tensor"),
        P("tensor"),
        P(None, "tensor"),
        P(("rollout", "tensor"), None, None, None),
        P(("rollout", "tensor"), None, None),
        P(None, "rollout", None, "tensor"),
        P("rollout"),
        P(),
    )
    return jax.shard_map(
        body, mesh=mesh, in_specs=placed, out_specs=P(None, "rollout", "tensor"), check_vma=False
    )
```

time: 322 us -> 167 us (0.52)
  Pallas kernels: 0 us -> 154 us
  waiting for transfers between devices: 144 us -> 0 us
  matrix products: 89.9 us -> 0 us
  local copies, waits for them, and re-layouts: 58.1 us -> 11.1 us
  between operations: 18.1 us -> 0.03 us
  other arithmetic: 11.2 us -> 0 us
    pallas_call x0 -> x2, Pallas kernels: none -> 154 us  [the longest x1 111 us: body(): pl.pallas_call(gather_merge_project, out_shape=(jax.ShapeDtypeStruct((ROW...]
    psum x1 -> x0, waiting for transfers between devices: 142 us -> none  [spread(): return lax.psum(jnp.where(mine, shard, jnp.zeros_like(shard)), axis)]
    dot_general x22 -> x0, matrix products: 89.9 us -> none  [the longest x4 43.3 us: project(): return jnp.dot(received, merged, preferred_element_type=jnp.float32)]
    unnamed x78 -> x11, local copies, waits for them, and re-layouts: 31.2 us -> 11.1 us
    slice x16 -> x0, local copies, waits for them, and re-layouts: 15 us -> none  [the longest x1 10.2 us: body(): base_parts = [w_query, w_keyval[:, 0], w_keyval[:, 1]]]
    squeeze x4 -> x0, local copies, waits for them, and re-layouts: 4.93 us -> none  [the longest x2 2.87 us: body(): factor_up[0, :, span_starts[member]:span_starts[member] + span_sizes[memb...]
    select_n x2 -> x0, other arithmetic: 4.29 us -> none  [spread(): return lax.psum(jnp.where(mine, shard, jnp.zeros_like(shard)), axis)]
  transfers between devices with their start and end apart: 5 -> 0, of which waited for: 1 -> 0; matrix products, arithmetic and copies ran while one was open for 29% -> 0% of each run, Pallas kernels for 0% -> 0%
where the time goes in v1:
time: 167 us; the launch traced here: 165 us
  Pallas kernels  154 us (92%)
  local copies, waits for them, and re-layouts  11.1 us (7%)
    pallas_call x1, Pallas kernels, body(): pl.pallas_call(gather_merge_project, out_shape=(jax.ShapeDtypeStruct((ROW...  111 us
    pallas_call x1, Pallas kernels, body(): pl.pallas_call(attend, grid=(ROWS // BLOCK,), out_shape=jax.ShapeDtypeStr...  43.2 us
    unnamed x11, local copies, waits for them, and re-layouts  11.1 us

profile of v1, /device:TPU:1, one launch (start us, length us, event | category | flops | bytes accessed | tf_op | source)
XLA Modules:
  0.0 165.1 jit_solution(81915353235539546)
XLA Ops:
  0.0 4.7 %copy.13 = bf16[1024,8,2,128]{3,1,2,0:T(8,128)(2,1)} copy(bf16[1024,8,2,128]{3,2,1,0:T(2,128)(2,1)} %bitcast.8) | data formatting | bytes 8388608
  4.7 0.0 copy-start.4
  4.7 110.8 %shard_map.100 = (f32[128,16,128]{2,1,0:T(8,128)}, bf16[4,128,128]{2,1,0:T(8,128)(2,1)}, bf16[4,128,128]{2,1,0:T(8,128)(2,1)}) custom-call(s32[3]{0:T(128)} %owners_ref.1, bf16[4,128,1024]{2,1,0:T(8,128)(2,1)} %x_hbm.1, bf16[8192,512]{1,0:T(8,128)(2,1)} %wq_hbm.1, bf16[8192,256]{1,0:T(8,128)(2,1)} %bitcast.7, bf16[1,3,64,8192]{3,2,1,0:T(8,128)(2,1)} %down_hbm.1, ...), custom_call_target="tpu_custom_call" | custom-call | tf_op jit(solution)/shard_map/pallas_call | solution.py:513
  115.5 0.0 copy-done.4
  115.5 0.0 copy-start
  115.5 3.4 %copy-done = bf16[2,128,128,128]{3,2,1,0:T(8,128)(2,1)S(1)} copy-done((bf16[2,128,128,128]{3,2,1,0:T(8,128)(2,1)S(1)}, bf16[2,128,128,128]{3,2,1,0:T(8,128)(2,1)}, u32[]{:S(2)}) %copy-start) | copy-done | bytes 8388632
  118.9 0.0 copy-start.1
  118.9 1.2 copy-done.1
  120.1 0.0 copy-start.2
  120.1 0.9 copy-done.2
  121.0 0.0 copy-start.3
  121.0 0.9 copy-done.3
  121.9 43.2 %shard_map.101 = bf16[4,128,512]{2,1,0:T(8,128)(2,1)} custom-call(s32[128]{0:T(128)S(1)} %copy-done.4, f32[128,16,128]{2,1,0:T(8,128)S(1)} %copy-done.1, bf16[4,128,128]{2,1,0:T(8,128)(2,1)S(1)} %copy-done.2, bf16[4,128,128]{2,1,0:T(8,128)(2,1)S(1)} %copy-done.3, bf16[2,128,128,128]{3,2,1,0:T(8,128)(2,1)S(1)} %copy-done), custom_call_target="tpu_custom_call" | custom-call | tf_op jit(solution)/shard_map/pallas_call | solution.py:555
Async XLA Ops:
  4.7 110.8 %copy-start.4 = (s32[128]{0:T(128)S(1)}, s32[128]{0:T(128)}, u32[]{:S(2)}) copy-start(s32[128]{0:T(128)} %len_ref.1) | copy-start | bytes 1540
  115.5 3.4 %copy-start = (bf16[2,128,128,128]{3,2,1,0:T(8,128)(2,1)S(1)}, bf16[2,128,128,128]{3,2,1,0:T(8,128)(2,1)}, u32[]{:S(2)}) copy-start(bf16[2,128,128,128]{3,2,1,0:T(8,128)(2,1)} %cache_ref.1) | copy-start | bytes 25165828
  118.9 1.2 copy-start.1
  120.1 0.9 copy-start.2
  121.0 0.9 copy-start.3

commit v2 on v1

v2 whole, which is shorter than its diff:
```python
import functools
import math

import jax
import jax.numpy as jnp
from jax import lax
from jax.experimental import pallas as pl
from jax.experimental.pallas import tpu as pltpu
from jax.sharding import PartitionSpec as P

MESH = pl.DeviceIdType.MESH
HD = 128
STEPS = 4
ROWS = 128
TOK = STEPS * ROWS
D = 8192
PART = 1024
RANK = 64
HALF = RANK // 2
QW = 512
KW = 128
QFULL = 4096
KFULL = 1024
NSEM = 190
CROSS = (512, 640)
BF = jnp.bfloat16
F32 = jnp.float32


ORDER = [
    ("f_core", 1), ("f_core", 0), ("f_core", 2), ("f_core", 3), ("zu", 2), ("zd", 2), ("xx", 2),
    ("c_tables", 0), ("f_second", 1), ("c_tables", 1), ("c_tables", 2), ("zu", 3), ("zd", 3),
    ("xx", 3), ("c_tables", 3), ("f_second", 0), ("c_split", 0), ("c_split", 1), ("zu", 4),
    ("zd", 4), ("xx", 4), ("c_split", 2), ("f_second", 2), ("c_split", 3), ("zu", 5), ("zd", 5),
    ("xx", 5), ("f_second", 3), ("zu", 6), ("zd", 6), ("xx", 6), ("f_third", 1), ("f_third", 0),
    ("f_third", 2), ("xx", 7), ("f_third", 3), ("zu", 7), ("zd", 7), ("f_ra", 0), ("f_ra", 1),
    ("xx", 8), ("zu", 8), ("zd", 8), ("f_ra", 2), ("zu", 9), ("zd", 9), ("xx", 9), ("xx", 10),
    ("f_ra", 3), ("f_rb", 1), ("f_rb", 0), ("zu", 10), ("zd", 10), ("xx", 11), ("f_rb", 2),
    ("zu", 11), ("zd", 11), ("xx", 12), ("f_rb", 3), ("f_sb", 1), ("zu", 12), ("f_sb", 0),
    ("xx", 13), ("f_sb", 2), ("xx", 14), ("zd", 12), ("f_sb", 3), ("f_sa", 1), ("xx", 15),
    ("zu", 13), ("zd", 13), ("xx", 16), ("xx", 17), ("f_sa", 0), ("zu", 14), ("f_sa", 3),
    ("zd", 14), ("f_sa", 2), ("xx", 18), ("xx", 19), ("f_yf", 1), ("zu", 15), ("xx", 20),
    ("zd", 15), ("xx", 21), ("f_yf", 0), ("zu", 16), ("xx", 22), ("zd", 16), ("xx", 23), ("zu", 17),
    ("zd", 17), ("xx", 24), ("f_yf", 3), ("zu", 18), ("zd", 18), ("xx", 25), ("zu", 19), ("zd", 19),
    ("xx", 26), ("f_yf", 2), ("xx", 27), ("zu", 20), ("f_last", 1), ("f_own", 1), ("f_near", 1),
    ("zd", 20), ("xx", 28), ("zu", 21), ("f_last", 0), ("f_end", 1), ("f_own", 0), ("f_near", 0),
    ("zd", 21), ("xx", 29), ("f_last", 3), ("f_end", 0), ("f_own", 3), ("f_near", 3), ("zu", 22),
    ("xx", 30), ("zd", 22), ("f_last", 2), ("f_own", 2), ("f_near", 2), ("f_end", 3), ("zu", 23),
    ("xx", 31), ("zd", 23), ("x_end", 0), ("x_end", 1), ("f_end", 2), ("c_merge_q", 0),
    ("c_merge_q", 1), ("c_merge_q", 2), ("c_merge_q", 3), ("x_end", 2), ("c_merge_kv", 0),
    ("c_merge_kv", 1), ("c_merge_kv", 2), ("c_merge_kv", 3), ("c_project", 0), ("c_project", 1),
    ("c_project", 2), ("c_project", 3), ("c_project", 4), ("c_project", 5), ("c_project", 6),
    ("c_project", 7),
]


def coordinates():
    rollout = lax.axis_index("rollout")
    tensor = lax.axis_index("tensor")
    core = rollout % 2
    x = (tensor // 4) * 2 + (rollout // 2) % 2
    return core, x, rollout // 4, tensor % 4


def device(core, x, y, z):
    return ((y * 2 + x % 2) * 2 + core, (x // 2) * 4 + z)


def decode(
    owners_ref,
    x_hbm,
    wq_hbm,
    wkv_hbm,
    down_hbm,
    up_hbm,
    bq_ref,
    bkv_ref,
    len_ref,
    rows_ref,
    cache_hbm,
    o_ref,
    q_ref,
    k_ref,
    v_ref,
    cache_ref,
    recent,
    recent_probs,
    probs,
    xs,
    wq,
    wkv,
    mkv,
    pairs,
    upstage,
    held,
    rcore,
    ry,
    yq,
    rz,
    rx,
    fac,
    upkv,
    acc,
    cos_ref,
    sin_ref,
    send,
    recv,
    local,
):
    core, x, y, z = coordinates()
    tensor = (x // 2) * 4 + z
    me = ((y * 2 + x % 2) * 2 + core) * 8 + tensor

    def at(dc=0, dx=0, dy=0, dz=0):
        return device((core + dc) % 2, (x + dx) % 4, (y + dy) % 4, (z + dz) % 4)

    z_up, z_down, z_far = at(dz=1), at(dz=3), at(dz=2)
    x_far = at(dx=2)
    y_up, y_down = at(dy=1), at(dy=3)
    other = at(dc=1)
    partners = [z_up, z_down, z_far, at(dx=1), x_far, at(dx=3), y_up, y_down, other]

    locals_used = [0]

    def fetch(src, dst):
        copy = pltpu.make_async_copy(src, dst, local.at[locals_used[0]])
        locals_used[0] += 1
        copy.start()
        return copy

    mine = pl.multiple_of(core * HALF, HALF)
    theirs = pl.multiple_of((1 - core) * HALF, HALF)
    rows = pl.ds(mine, HALF)

    barrier = pltpu.get_barrier_semaphore()
    for partner in partners:
        pl.semaphore_signal(barrier, inc=1, device_id=partner, device_id_type=MESH)
    ups = []
    for t in range(8):
        ups.append(fetch(up_hbm.at[0, :, pl.ds(t * QW, QW)], upstage.at[:, pl.ds(t * PART, QW)]))
        for j in range(2):
            ups.append(
                fetch(
                    up_hbm.at[0, :, pl.ds(QFULL + j * KFULL + t * KW, KW)],
                    upstage.at[:, pl.ds(t * PART + QW + j * KW, KW)],
                )
            )
    down_load = fetch(down_hbm.at[0, :, rows], held)
    for t in range(8):
        upstage[:, pl.ds(t * PART + QW + 2 * KW, PART - QW - 2 * KW)] = jnp.zeros(
            (RANK, PART - QW - 2 * KW), BF
        )
    pl.semaphore_wait(barrier, len(partners))

    used = [0]

    def put(src, dst, target):
        index = used[0]
        used[0] += 1
        copy = pltpu.make_async_remote_copy(
            src_ref=src,
            dst_ref=dst,
            send_sem=send.at[index],
            recv_sem=recv.at[index],
            device_id=target,
            device_id_type=MESH,
        )
        copy.start()
        return copy

    started = []
    arrived = set()

    def land(copy):
        if id(copy) not in arrived:
            arrived.add(id(copy))
            copy.wait_recv()

    def push(src, target, dst=None):
        copy = put(src, src if dst is None else dst, target)
        started.append(copy)
        return copy

    def chunk(t, p, columns=(0, PART)):
        piece = xs.at[t, p // 2, pl.ds((p % 2) * 64, 64)]
        if columns == (0, PART):
            return piece
        return piece.at[:, pl.ds(columns[0], columns[1] - columns[0])]

    def own(p):
        return x_hbm.at[p // 2, pl.ds((p % 2) * 64, 64)]

    base = (x // 2) * 4
    far_base = 4 - base
    far_slot = far_base + z
    z_prev, z_next, z_opp = (z + 3) % 4, (z + 1) % 4, (z + 2) % 4

    def across(member):
        return push(down_hbm.at[0, member - 1, pl.ds(theirs, HALF)], other, rcore.at[member])

    core_copies = {1: across(1)}

    got = {}

    def near_part(p):
        return (0, CROSS[p % 2])

    def far_part(p):
        return (CROSS[p % 2], PART)

    up_list = [("own", p) for p in range(8)]
    up_list += [("far", p) for p in range(4)] + [("ring", p) for p in range(4)]
    up_list += [("far", p) for p in range(4, 8)] + [("farring", p) for p in range(4)]

    def z_send(direction, i):
        kind, p = up_list[i]
        if direction < 0:
            p = (p + 4) % 8
        target, behind = (z_up, z_prev) if direction > 0 else (z_down, z_next)
        if kind == "own":
            copy = push(own(p), target, chunk(tensor, p))
        elif kind == "far":
            land(got["x", p])
            copy = push(chunk(far_slot, p, near_part(p)), target)
        elif kind == "ring":
            land(got[direction, "own", p])
            copy = push(chunk(base + behind, p), target)
        else:
            land(got[direction, "far", p])
            copy = push(chunk(far_base + behind, p, near_part(p)), target)
        got[direction, kind, p] = copy

    def zu(i):
        z_send(1, i)

    def zd(i):
        z_send(-1, i)

    x_list = [("own", p) for p in (0, 4, 1, 5, 2, 6, 3, 7)]
    for p in range(4):
        x_list += [("prev", p), ("next", p + 4)]
    for p in range(4):
        x_list += [("prev", p + 4), ("next", p)]
    for p in range(4):
        x_list += [("opp", p), ("opp", p + 4)]

    def xx(i):
        kind, p = x_list[i]
        if kind == "own":
            got["x", p] = push(own(p), x_far, chunk(tensor, p))
            return
        if kind == "prev":
            slot, arrival = base + z_prev, got[1, "own", p]
        elif kind == "next":
            slot, arrival = base + z_next, got[-1, "own", p]
        else:
            slot, arrival = base + z_opp, got[1 if p < 4 else -1, "ring", p]
        land(arrival)
        got["x", kind, p] = push(chunk(slot, p, far_part(p)), x_far)

    def x_end(part):
        for p in range(8):
            if part == 0:
                land(got["x", "prev", p])
                land(got[1, "far", p])
            elif part == 1:
                land(got["x", "next", p])
                land(got[-1, "far", p])
            else:
                land(got["x", "opp", p])
                land(got[1 if p < 4 else -1, "farring", p])

    for i in range(2):
        zu(i)
        zd(i)
        xx(i)
    for copy in ups:
        copy.wait()
    core_copies[0] = push(upstage.at[pl.ds(theirs, HALF)], other, rcore.at[0])
    for member in (2, 3):
        core_copies[member] = across(member)
    x_load = fetch(x_hbm, xs.at[tensor])
    wkv_load = fetch(wkv_hbm, wkv)
    wq_load = fetch(wq_hbm, wq)
    cache_load = fetch(cache_hbm, cache_ref)
    down_load.wait()

    def c_tables(s):
        lane = lax.broadcasted_iota(jnp.int32, (ROWS, HD), 1)
        frequency = jnp.exp(
            -((lane % (HD // 2)).astype(F32) * (2.0 / HD)) * math.log(1000000.0)
        )
        lengths = jnp.broadcast_to(len_ref[...], (ROWS, HD)).astype(F32).T
        sign = jnp.where(lane < HD // 2, -1.0, 1.0)
        angles = (lengths + float(s)) * frequency
        cos_ref[pl.ds(s * ROWS, ROWS), :] = jnp.cos(angles)
        sin_ref[pl.ds(s * ROWS, ROWS), :] = jnp.sin(angles) * sign

    me_other = ((y * 2 + x % 2) * 2 + 1 - core) * 8 + tensor
    keep = [(owners_ref[m] == me).astype(F32).astype(BF) for m in range(3)]
    take = [(owners_ref[m] == me_other).astype(F32).astype(BF) for m in range(3)]

    def quarter(q):
        return pl.ds(pl.multiple_of(q * 2048, 2048), 2048)

    y_opp, y_next, y_prev = (y + 2) % 4, (y + 1) % 4, (y + 3) % 4
    low_rows, high_rows = pl.ds(0, HALF // 2), pl.ds(HALF // 2, HALF // 2)
    fac_low = pl.ds(mine, HALF // 2)
    fac_high = pl.ds(pl.multiple_of(mine + HALF // 2, HALF // 2), HALF // 2)
    state = {}

    def f_core(m):
        land(core_copies[m])
        if m == 0:
            spans = [(0, 0, QW), (1, QW, KW), (2, QW + KW, KW)]
        else:
            spans = [(m - 1, 0, PART)]

        def add_block(t, carry):
            start = pl.multiple_of(t * PART, PART)
            for owner, offset, width in spans:
                columns = pl.ds(start + offset, width)
                here = upstage[rows, columns] if m == 0 else held[m - 1, :, columns]
                rcore[m, :, columns] = here * keep[owner] + rcore[m, :, columns] * take[owner]
            return carry

        lax.fori_loop(0, 8, add_block, 0)
        state["first", m] = [
            push(rcore.at[m, low_rows, quarter(y_opp)], y_up, ry.at[m, 0]),
            push(rcore.at[m, high_rows, quarter(y_opp)], y_down, ry.at[m, 1]),
        ]
        state["raw", m] = [
            push(rcore.at[m, low_rows, quarter(y_prev)], y_down, ry.at[m, 2]),
            push(rcore.at[m, high_rows, quarter(y_next)], y_up, ry.at[m, 3]),
        ]

    def f_second(m):
        land(state["first", m][0])
        ry[m, 0] = ry[m, 0] + rcore[m, low_rows, quarter(y_next)]
        state["raw", m].append(push(ry.at[m, 0], y_up, ry.at[m, 4]))
        land(state["first", m][1])
        ry[m, 1] = ry[m, 1] + rcore[m, high_rows, quarter(y_prev)]
        state["raw", m].append(push(ry.at[m, 1], y_down, ry.at[m, 5]))

    def wait_all(copies):
        for copy in copies:
            land(copy)

    def first_at(m, d):
        return at(dz=d) if m % 2 == 0 else at(dx=d)

    def second_at(m, d):
        return at(dx=d) if m % 2 == 0 else at(dz=d)

    def places(m):
        return (z, x) if m % 2 == 0 else (x, z)

    def wide(index):
        return pl.ds(pl.multiple_of(index * 512, 512), 512)

    def narrow(index):
        return pl.ds(pl.multiple_of(index * 128, 128), 128)

    def f_third(m):
        wait_all(state["raw", m])
        yq[m, low_rows] = rcore[m, low_rows, quarter(y)] + ry[m, 2] + ry[m, 4]
        yq[m, high_rows] = rcore[m, high_rows, quarter(y)] + ry[m, 3] + ry[m, 5]
        outer = places(m)[0]
        state["ra", m] = [
            push(yq.at[m, :, wide((outer + d) % 4)], first_at(m, d), rz.at[m, d - 1])
            for d in (1, 2, 3)
        ]

    def f_ra(m):
        wait_all(state["ra", m])
        outer, inner = places(m)
        rz[m, 3] = yq[m, :, wide(outer)] + rz[m, 0] + rz[m, 1] + rz[m, 2]
        state["rb", m] = [
            push(rz.at[m, 3, :, narrow((inner + d) % 4)], second_at(m, d), rx.at[m, d - 1])
            for d in (1, 2, 3)
        ]

    def f_rb(m):
        wait_all(state["rb", m])
        outer, inner = places(m)
        rx[m, 3] = rz[m, 3, :, narrow(inner)] + rx[m, 0] + rx[m, 1] + rx[m, 2]
        span = pl.ds(pl.multiple_of(y * 2048 + outer * 512 + inner * 128, 128), 128)
        state["sb", m] = [
            push(rx.at[m, 3], second_at(m, d), fac.at[m, rows, span]) for d in (1, 2, 3)
        ]
        fac[m, rows, span] = rx[m, 3]

    def f_sb(m):
        wait_all(state["sb", m])
        outer = places(m)[0]
        piece = fac.at[m, rows, pl.ds(pl.multiple_of(y * 2048 + outer * 512, 512), 512)]
        state["sa", m] = [push(piece, first_at(m, d)) for d in (1, 2, 3)]

    def f_sa(m):
        wait_all(state["sa", m])
        piece = fac.at[m, rows, quarter(y)]
        state["ys", m] = [push(piece, y_up), push(piece, y_down), push(piece, other)]

    def f_yf(m):
        land(state["ys", m][0])
        up = push(fac.at[m, fac_low, quarter(y_prev)], y_up)
        down_core = push(fac.at[m, rows, quarter(y_prev)], other)
        land(state["ys", m][1])
        down = push(fac.at[m, fac_high, quarter(y_next)], y_down)
        up_core = push(fac.at[m, rows, quarter(y_next)], other)
        state["yf", m] = [up, down, down_core, up_core]

    def f_last(m):
        wait_all(state["yf", m][:2])
        state["yl", m] = push(fac.at[m, rows, quarter(y_opp)], other)

    def f_own(m):
        land(state["ys", m][2])

    def f_near(m):
        wait_all(state["yf", m][2:])

    def f_end(m):
        land(state["yl", m])

    def c_split(part):
        if part == 0:
            wkv_load.wait()

        def split_pairs(i, carry):
            pairs[...] = wkv[pl.ds(pl.multiple_of(i * 1024, 1024), 1024), :].astype(F32)
            ks = pl.ds(pl.multiple_of(i * 512, 512), 512)
            for j in range(2):
                mkv[ks, pl.ds(j * KW, KW)] = pairs[pl.ds(j, 512, stride=2), :].astype(BF)
            return carry

        lax.fori_loop(part * 4, part * 4 + 4, split_pairs, 0)

    up_columns = pl.multiple_of(tensor * PART, PART)
    block = 512
    quarters = [y, y_prev, y_next, y_opp]

    def c_merge_q(part):
        if part == 0:
            wq_load.wait()

        def merge(i, carry):
            ks = pl.ds(pl.multiple_of(quarters[part] * 2048 + i * block, block), block)
            low = lax.dot_general(
                fac[1, :, ks],
                fac[0, :, pl.ds(up_columns, QW)],
                (((0,), (0,)), ((), ())),
                preferred_element_type=F32,
            )
            wq[ks, :] = (wq[ks, :].astype(F32) + low).astype(BF)
            return carry

        lax.fori_loop(0, 4, merge, 0)

    def c_merge_kv(part):
        if part == 0:
            upkv[...] = jnp.zeros_like(upkv)
            for j in range(2):
                upkv[pl.ds(j * RANK, RANK), pl.ds(j * KW, KW)] = fac[
                    0, :, pl.ds(up_columns + QW + j * KW, KW)
                ]

        def merge(i, carry):
            ks = pl.ds(pl.multiple_of(quarters[part] * 2048 + i * block, block), block)
            low = lax.dot_general(
                fac[pl.ds(2, 2), :, ks].reshape(2 * RANK, block),
                upkv[...],
                (((0,), (0,)), ((), ())),
                preferred_element_type=F32,
            )
            mkv[ks, :] = (mkv[ks, :].astype(F32) + low).astype(BF)
            return carry

        lax.fori_loop(0, 4, merge, 0)

    sources = [
        tensor, base + z_prev, base + z_next, base + z_opp,
        far_slot, far_base + z_prev, far_base + z_next, far_base + z_opp,
    ]

    def c_project(part):
        t = sources[part]
        if part == 0:
            x_load.wait()
        ks = pl.ds(pl.multiple_of(t * PART, PART), PART)
        received = xs[t].reshape(TOK, PART)
        query = jnp.dot(received, wq[ks, :], preferred_element_type=F32)
        keyval = jnp.dot(received, mkv[ks, :], preferred_element_type=F32)
        if part == 0:
            acc[:, pl.ds(0, QW)] = query
            acc[:, pl.ds(QW, 2 * KW)] = keyval
        else:
            acc[:, pl.ds(0, QW)] += query
            acc[:, pl.ds(QW, 2 * KW)] += keyval

    steps = dict(
        f_core=f_core, f_second=f_second, f_third=f_third, f_ra=f_ra, f_rb=f_rb, f_sb=f_sb, f_sa=f_sa,
        f_yf=f_yf, f_last=f_last, f_own=f_own, f_near=f_near, f_end=f_end,
        zu=zu, zd=zd, xx=xx, x_end=x_end, c_tables=c_tables, c_split=c_split, c_merge_q=c_merge_q, c_merge_kv=c_merge_kv,
        c_project=c_project,
    )
    for name, index in ORDER:
        steps[name](index)

    def rotate(vectors, token_rows):
        return vectors * cos_ref[token_rows, :] + pltpu.roll(vectors, HD // 2, 1) * sin_ref[token_rows, :]

    for s in range(STEPS):
        token_rows = pl.ds(s * ROWS, ROWS)
        for h in range(QW // HD):
            columns = pl.ds(h * HD, HD)
            turned = rotate(acc[token_rows, columns] + bq_ref[:, columns], token_rows)
            q_ref[:, s * 4 + h, :] = turned.astype(BF).astype(F32)
        turned = rotate(acc[token_rows, pl.ds(QW, KW)] + bkv_ref[pl.ds(0, 1), :], token_rows)
        k_ref[s] = turned.astype(BF)
        v_ref[s] = (acc[token_rows, pl.ds(QW + KW, KW)] + bkv_ref[pl.ds(1, 1), :]).astype(BF)

    cache_load.wait()

    def attend_block(i, carry):
        attend(
            pl.multiple_of(i * BLOCK, BLOCK), rows_ref, q_ref, k_ref, v_ref, cache_ref, o_ref,
            recent, recent_probs, probs,
        )
        return carry

    lax.fori_loop(0, ROWS // BLOCK, attend_block, 0)
    for copy in started:
        land(copy)
        copy.wait_send()


BLOCK = 32


def attend(first, len_ref, q_ref, k_ref, v_ref, cache_ref, o_ref, recent, recent_probs, probs):
    rows = pl.ds(first, BLOCK)
    queries = q_ref[rows].reshape(BLOCK * 16, HD).astype(BF)
    keys = k_ref[:, rows, :].reshape(BLOCK * STEPS, HD)
    scale = 1.0 / math.sqrt(HD)
    scores = (
        lax.dot_general(queries, keys, (((1,), (1,)), ((), ())), preferred_element_type=F32) * scale
    )
    row = lax.broadcasted_iota(jnp.int32, scores.shape, 0)
    lane = lax.broadcasted_iota(jnp.int32, scores.shape, 1)
    valid = (row // 16 == lane % BLOCK) & (lane // BLOCK <= (row // 4) % 4)
    recent[...] = jnp.where(valid, scores, -1e30)
    slots = lax.broadcasted_iota(jnp.int32, (16, HD), 1)
    for r in range(BLOCK):
        raw = lax.dot_general(
            q_ref[first + r].astype(BF),
            cache_ref[0, first + r],
            (((1,), (1,)), ((), ())),
            preferred_element_type=F32,
        )
        q_ref[first + r] = jnp.where(slots < len_ref[first + r], raw * scale, -1e30)
    for part in range(4):
        group = pl.ds(first + part * BLOCK // 4, BLOCK // 4)
        mine = pl.ds(part * BLOCK * 4, BLOCK * 4)
        cached = q_ref[group].reshape(BLOCK * 4, HD)
        fresh = recent[mine, :]
        top = jnp.max(jnp.maximum(cached, fresh), axis=1, keepdims=True)
        cached = jnp.exp(cached - top)
        fresh = jnp.exp(fresh - top)
        total = jnp.sum(cached + fresh, axis=1, keepdims=True)
        recent_probs[mine, :] = (fresh / total).astype(BF)
        probs[mine, :] = (cached / total).astype(BF)
    for r in range(BLOCK):
        q_ref[first + r] = jnp.dot(
            probs[pl.ds(r * 16, 16), :], cache_ref[1, first + r], preferred_element_type=F32
        )
    values = v_ref[:, rows, :].reshape(BLOCK * STEPS, HD)
    q_ref[rows] += jnp.dot(recent_probs[...], values, preferred_element_type=F32).reshape(
        BLOCK, 16, HD
    )
    for s in range(STEPS):
        for h in range(4):
            o_ref[s, rows, pl.ds(h * HD, HD)] = q_ref[rows, s * 4 + h, :].astype(BF)


def body(
    inputs,
    w_query,
    w_keyval,
    bias_query,
    bias_keyval,
    factor_down,
    factor_up,
    cache,
    lengths,
    owners,
):
    any_space = pl.BlockSpec(memory_space=pl.ANY)
    vmem = pl.BlockSpec(memory_space=pltpu.VMEM)
    smem = pl.BlockSpec(memory_space=pltpu.SMEM)
    return pl.pallas_call(
        decode,
        out_shape=jax.ShapeDtypeStruct((STEPS, ROWS, QW), BF),
        in_specs=[smem] + [any_space] * 5 + [vmem] * 3 + [smem, any_space],
        out_specs=vmem,
        scratch_shapes=[
            pltpu.VMEM((ROWS, 16, HD), F32),
            pltpu.VMEM((STEPS, ROWS, HD), BF),
            pltpu.VMEM((STEPS, ROWS, HD), BF),
            pltpu.VMEM((2, ROWS, HD, HD), BF),
            pltpu.VMEM((BLOCK * 16, HD), F32),
            pltpu.VMEM((BLOCK * 16, HD), BF),
            pltpu.VMEM((BLOCK * 16, HD), BF),
            pltpu.VMEM((8, STEPS, ROWS, PART), BF),
            pltpu.VMEM((D, QW), BF),
            pltpu.VMEM((2 * D, KW), BF),
            pltpu.VMEM((D, 2 * KW), BF),
            pltpu.VMEM((1024, KW), F32),
            pltpu.VMEM((RANK, D), BF),
            pltpu.VMEM((3, HALF, D), BF),
            pltpu.VMEM((4, HALF, D), BF),
            pltpu.VMEM((4, 6, HALF // 2, 2048), BF),
            pltpu.VMEM((4, HALF, 2048), BF),
            pltpu.VMEM((4, 4, HALF, 512), BF),
            pltpu.VMEM((4, 4, HALF, 128), BF),
            pltpu.VMEM((4, RANK, D), BF),
            pltpu.VMEM((2 * RANK, 2 * KW), BF),
            pltpu.VMEM((TOK, QW + 2 * KW), F32),
            pltpu.VMEM((TOK, HD), F32),
            pltpu.VMEM((TOK, HD), F32),
            pltpu.SemaphoreType.DMA((NSEM,)),
            pltpu.SemaphoreType.DMA((NSEM,)),
            pltpu.SemaphoreType.DMA((32,)),
        ],
        compiler_params=pltpu.CompilerParams(
            collective_id=0, has_side_effects=True, vmem_limit_bytes=58 << 20
        ),
    )(
        owners,
        inputs,
        w_query,
        w_keyval.reshape(2 * D, KW),
        factor_down,
        factor_up,
        bias_query.reshape(1, QW),
        bias_keyval,
        lengths.reshape(1, ROWS),
        lengths,
        cache,
    )


def solution(mesh):
    placed = (
        P(None, "rollout", "tensor"),
        P(None, "tensor"),
        P(None, None, "tensor"),
        P("tensor"),
        P(None, "tensor"),
        P(("rollout", "tensor"), None, None, None),
        P(("rollout", "tensor"), None, None),
        P(None, "rollout", None, "tensor"),
        P("rollout"),
        P(),
    )
    return jax.shard_map(
        body, mesh=mesh, in_specs=placed, out_specs=P(None, "rollout", "tensor"), check_vma=False
    )
```

time: 167 us -> 94.8 us (0.57); the launches traced: 165 us -> 94.6 us
  Pallas kernels: 154 us -> 92.7 us
  local copies, waits for them, and re-layouts: 11.1 us -> 1.87 us
    pallas_call x2 -> x1, Pallas kernels: 154 us -> 92.7 us  [body(): pl.pallas_call(decode, out_shape=jax.ShapeDtypeStruct((STEPS, ROWS, QW),...]
    unnamed x11 -> x1, local copies, waits for them, and re-layouts: 11.1 us -> 1.87 us
where the time goes in v2:
time: 94.8 us; the launch traced here: 94.6 us
  Pallas kernels  92.7 us (98%)
  local copies, waits for them, and re-layouts  1.87 us (2%)
    pallas_call x1, Pallas kernels, body(): pl.pallas_call(decode, out_shape=jax.ShapeDtypeStruct((STEPS, ROWS, QW),...  92.7 us

profile of v2, /device:TPU:1, one launch (start us, length us, event | category | flops | bytes accessed | tf_op | source)
XLA Modules:
  0.0 94.6 jit_solution(3037980518482173269)
XLA Ops:
  0.0 92.7 %shard_map.100 = bf16[4,128,512]{2,1,0:T(8,128)(2,1)} custom-call(s32[3]{0:T(128)} %owners_ref.1, bf16[4,128,1024]{2,1,0:T(8,128)(2,1)} %x_hbm.1, bf16[8192,512]{1,0:T(8,128)(2,1)} %wq_hbm.1, bf16[16384,128]{1,0:T(8,128)(2,1)} %bitcast.3, bf16[1,3,64,8192]{3,2,1,0:T(8,128)(2,1)} %down_hbm.1, bf16[1,64,6144]{2,1,0:T(8,128)(2,1)} %up_hbm.1, f32[1,512]{1,0:T(1,128)} %bitcast.5, ...), custom_call_target="tpu_custom_call" | custom-call | tf_op jit(solution)/shard_map/pallas_call | solution.py:601
  92.7 1.9 %copy.12 = bf16[4,128,512]{2,1,0:T(8,128)(2,1)} copy(bf16[4,128,512]{2,1,0:T(8,128)(2,1)} %shard_map.100) | data formatting | bytes 1048576

commit v3 on v2

--- a/solution.py
+++ b/solution.py
@@ -15,6 +15,7 @@
 TOK = STEPS * ROWS
 D = 8192
 PART = 1024
+SUB = 256
 RANK = 64
 HALF = RANK // 2
 QW = 512
@@ -28,29 +29,27 @@
 
 
 ORDER = [
-    ("f_core", 1), ("f_core", 0), ("f_core", 2), ("f_core", 3), ("zu", 2), ("zd", 2), ("xx", 2),
-    ("c_tables", 0), ("f_second", 1), ("c_tables", 1), ("c_tables", 2), ("zu", 3), ("zd", 3),
-    ("xx", 3), ("c_tables", 3), ("f_second", 0), ("c_split", 0), ("c_split", 1), ("zu", 4),
-    ("zd", 4), ("xx", 4), ("c_split", 2), ("f_second", 2), ("c_split", 3), ("zu", 5), ("zd", 5),
-    ("xx", 5), ("f_second", 3), ("zu", 6), ("zd", 6), ("xx", 6), ("f_third", 1), ("f_third", 0),
-    ("f_third", 2), ("xx", 7), ("f_third", 3), ("zu", 7), ("zd", 7), ("f_ra", 0), ("f_ra", 1),
-    ("xx", 8), ("zu", 8), ("zd", 8), ("f_ra", 2), ("zu", 9), ("zd", 9), ("xx", 9), ("xx", 10),
-    ("f_ra", 3), ("f_rb", 1), ("f_rb", 0), ("zu", 10), ("zd", 10), ("xx", 11), ("f_rb", 2),
-    ("zu", 11), ("zd", 11), ("xx", 12), ("f_rb", 3), ("f_sb", 1), ("zu", 12), ("f_sb", 0),
-    ("xx", 13), ("f_sb", 2), ("xx", 14), ("zd", 12), ("f_sb", 3), ("f_sa", 1), ("xx", 15),
-    ("zu", 13), ("zd", 13), ("xx", 16), ("xx", 17), ("f_sa", 0), ("zu", 14), ("f_sa", 3),
-    ("zd", 14), ("f_sa", 2), ("xx", 18), ("xx", 19), ("f_yf", 1), ("zu", 15), ("xx", 20),
-    ("zd", 15), ("xx", 21), ("f_yf", 0), ("zu", 16), ("xx", 22), ("zd", 16), ("xx", 23), ("zu", 17),
-    ("zd", 17), ("xx", 24), ("f_yf", 3), ("zu", 18), ("zd", 18), ("xx", 25), ("zu", 19), ("zd", 19),
-    ("xx", 26), ("f_yf", 2), ("xx", 27), ("zu", 20), ("f_last", 1), ("f_own", 1), ("f_near", 1),
-    ("zd", 20), ("xx", 28), ("zu", 21), ("f_last", 0), ("f_end", 1), ("f_own", 0), ("f_near", 0),
-    ("zd", 21), ("xx", 29), ("f_last", 3), ("f_end", 0), ("f_own", 3), ("f_near", 3), ("zu", 22),
-    ("xx", 30), ("zd", 22), ("f_last", 2), ("f_own", 2), ("f_near", 2), ("f_end", 3), ("zu", 23),
-    ("xx", 31), ("zd", 23), ("x_end", 0), ("x_end", 1), ("f_end", 2), ("c_merge_q", 0),
-    ("c_merge_q", 1), ("c_merge_q", 2), ("c_merge_q", 3), ("x_end", 2), ("c_merge_kv", 0),
-    ("c_merge_kv", 1), ("c_merge_kv", 2), ("c_merge_kv", 3), ("c_project", 0), ("c_project", 1),
-    ("c_project", 2), ("c_project", 3), ("c_project", 4), ("c_project", 5), ("c_project", 6),
-    ("c_project", 7),
+    ("f_core", 1), ("c_tables", 0), ("f_core", 0), ("f_core", 2), ("f_core", 3), ("zu", 2),
+    ("zd", 2), ("xx", 2), ("c_tables", 1), ("c_tables", 2), ("f_second", 1), ("c_tables", 3),
+    ("c_split", 0), ("zu", 3), ("zd", 3), ("xx", 3), ("c_split", 1), ("c_split", 2),
+    ("f_second", 0), ("c_split", 3), ("zu", 4), ("zd", 4), ("xx", 4), ("f_second", 2), ("zu", 5),
+    ("zd", 5), ("xx", 5), ("f_second", 3), ("zu", 6), ("zd", 6), ("xx", 6), ("f_third", 1),
+    ("f_third", 0), ("f_third", 2), ("xx", 7), ("f_third", 3), ("zu", 7), ("zd", 7), ("f_ra", 0),
+    ("f_ra", 1), ("zu", 8), ("f_ra", 2), ("zd", 8), ("xx", 8), ("zu", 9), ("zd", 9), ("xx", 9),
+    ("f_ra", 3), ("f_rb", 1), ("f_rb", 0), ("f_rb", 2), ("zu", 10), ("zd", 10), ("xx", 10),
+    ("zu", 11), ("zd", 11), ("xx", 11), ("f_rb", 3), ("f_sb", 1), ("f_sb", 2), ("xx", 12),
+    ("xx", 13), ("zu", 12), ("zd", 12), ("f_sb", 3), ("f_sa", 1), ("xx", 14), ("zu", 13),
+    ("zd", 13), ("f_sa", 2), ("xx", 15), ("c_merge_q", 0), ("xx", 16), ("zu", 14), ("zd", 14),
+    ("f_sa", 3), ("zu", 15), ("zu", 16), ("zd", 15), ("zd", 16), ("xx", 17), ("xx", 18), ("zu", 17),
+    ("zd", 17), ("xx", 19), ("xx", 20), ("xx", 21), ("xx", 22), ("f_yf", 1), ("xx", 23),
+    ("c_merge_kv", 0), ("zu", 18), ("zd", 18), ("xx", 24), ("zu", 19), ("zd", 19), ("xx", 25),
+    ("zu", 20), ("zd", 20), ("xx", 26), ("c_merge_q", 1), ("c_merge_q", 2), ("f_yf", 2), ("zu", 21),
+    ("zd", 21), ("xx", 27), ("xx", 28), ("zu", 22), ("zd", 22), ("xx", 29), ("f_yf", 3), ("zu", 23),
+    ("zd", 23), ("xx", 30), ("f_last", 1), ("c_merge_kv", 1), ("xx", 31), ("c_merge_kv", 2),
+    ("c_most", 0), ("c_most", 1), ("f_last", 2), ("c_merge_q", 3), ("x_end", 0), ("x_end", 1),
+    ("c_most", 2), ("f_last", 3), ("c_most", 3), ("c_most", 4), ("c_most", 5), ("c_merge_kv", 3),
+    ("c_most", 6), ("c_rest", 0), ("c_rest", 1), ("c_rest", 2), ("c_rest", 3), ("c_rest", 4),
+    ("c_rest", 5), ("c_rest", 6), ("x_end", 2), ("c_most", 7), ("c_rest", 7),
 ]
 
 
@@ -94,11 +93,14 @@
     upstage,
     held,
     rcore,
+    csum,
     ry,
     yq,
     rz,
     rx,
     fac,
+    ru,
+    uall,
     upkv,
     acc,
     cos_ref,
@@ -118,7 +120,8 @@
     x_far = at(dx=2)
     y_up, y_down = at(dy=1), at(dy=3)
     other = at(dc=1)
-    partners = [z_up, z_down, z_far, at(dx=1), x_far, at(dx=3), y_up, y_down, other]
+    y_all = [at(dc=c, dy=d) for c in range(2) for d in range(4) if c + d > 0]
+    partners = [z_up, z_down, z_far, at(dx=1), x_far, at(dx=3), *y_all]
 
     locals_used = [0]
 
@@ -311,35 +314,44 @@
 
     def f_core(m):
         land(core_copies[m])
-        if m == 0:
-            spans = [(0, 0, QW), (1, QW, KW), (2, QW + KW, KW)]
-        else:
-            spans = [(m - 1, 0, PART)]
 
         def add_block(t, carry):
             start = pl.multiple_of(t * PART, PART)
-            for owner, offset, width in spans:
-                columns = pl.ds(start + offset, width)
-                here = upstage[rows, columns] if m == 0 else held[m - 1, :, columns]
-                rcore[m, :, columns] = here * keep[owner] + rcore[m, :, columns] * take[owner]
+            block = t if m > 0 else (t % 4) * 2 + t // 4
+            place = pl.multiple_of(block * SUB, SUB)
+            for q in range(4):
+                if m > 0:
+                    spans = [(m - 1, 0, SUB)]
+                elif q < 2:
+                    spans = [(0, 0, SUB)]
+                else:
+                    spans = [(1, 0, KW), (2, KW, KW)]
+                for owner, offset, width in spans:
+                    target = pl.ds(place + q * 2048 + offset, width)
+                    if m == 0 and q == 3:
+                        csum[m, :, target] = jnp.zeros((HALF, width), BF)
+                        continue
+                    columns = pl.ds(start + q * SUB + offset, width)
+                    here = upstage[rows, columns] if m == 0 else held[m - 1, :, columns]
+                    csum[m, :, target] = here * keep[owner] + rcore[m, :, columns] * take[owner]
             return carry
 
         lax.fori_loop(0, 8, add_block, 0)
         state["first", m] = [
-            push(rcore.at[m, low_rows, quarter(y_opp)], y_up, ry.at[m, 0]),
-            push(rcore.at[m, high_rows, quarter(y_opp)], y_down, ry.at[m, 1]),
+            push(csum.at[m, low_rows, quarter(y_opp)], y_up, ry.at[m, 0]),
+            push(csum.at[m, high_rows, quarter(y_opp)], y_down, ry.at[m, 1]),
         ]
         state["raw", m] = [
-            push(rcore.at[m, low_rows, quarter(y_prev)], y_down, ry.at[m, 2]),
-            push(rcore.at[m, high_rows, quarter(y_next)], y_up, ry.at[m, 3]),
+            push(csum.at[m, low_rows, quarter(y_prev)], y_down, ry.at[m, 2]),
+            push(csum.at[m, high_rows, quarter(y_next)], y_up, ry.at[m, 3]),
         ]
 
     def f_second(m):
         land(state["first", m][0])
-        ry[m, 0] = ry[m, 0] + rcore[m, low_rows, quarter(y_next)]
+        ry[m, 0] = ry[m, 0] + csum[m, low_rows, quarter(y_next)]
         state["raw", m].append(push(ry.at[m, 0], y_up, ry.at[m, 4]))
         land(state["first", m][1])
-        ry[m, 1] = ry[m, 1] + rcore[m, high_rows, quarter(y_prev)]
+        ry[m, 1] = ry[m, 1] + csum[m, high_rows, quarter(y_prev)]
         state["raw", m].append(push(ry.at[m, 1], y_down, ry.at[m, 5]))
 
     def wait_all(copies):
@@ -361,10 +373,13 @@
     def narrow(index):
         return pl.ds(pl.multiple_of(index * 128, 128), 128)
 
+    def half_of(xx):
+        return pl.ds(pl.multiple_of((xx // 2) * SUB, SUB), SUB)
+
     def f_third(m):
         wait_all(state["raw", m])
-        yq[m, low_rows] = rcore[m, low_rows, quarter(y)] + ry[m, 2] + ry[m, 4]
-        yq[m, high_rows] = rcore[m, high_rows, quarter(y)] + ry[m, 3] + ry[m, 5]
+        yq[m, low_rows] = csum[m, low_rows, quarter(y)] + ry[m, 2] + ry[m, 4]
+        yq[m, high_rows] = csum[m, high_rows, quarter(y)] + ry[m, 3] + ry[m, 5]
         outer = places(m)[0]
         state["ra", m] = [
             push(yq.at[m, :, wide((outer + d) % 4)], first_at(m, d), rz.at[m, d - 1])
@@ -375,6 +390,11 @@
         wait_all(state["ra", m])
         outer, inner = places(m)
         rz[m, 3] = yq[m, :, wide(outer)] + rz[m, 0] + rz[m, 1] + rz[m, 2]
+        if m == 0:
+            state["rb", m] = [
+                push(rz.at[m, 3, :, half_of((x + d) % 4)], at(dx=d), ru.at[d - 1]) for d in (1, 2, 3)
+            ]
+            return
         state["rb", m] = [
             push(rz.at[m, 3, :, narrow((inner + d) % 4)], second_at(m, d), rx.at[m, d - 1])
             for d in (1, 2, 3)
@@ -382,6 +402,12 @@
 
     def f_rb(m):
         wait_all(state["rb", m])
+        if m == 0:
+            ru[3] = rz[m, 3, :, half_of(x)] + ru[0] + ru[1] + ru[2]
+            place = uall.at[rows, pl.ds(pl.multiple_of(y * SUB, SUB), SUB)]
+            state["u"] = [push(ru.at[3], device_id, place) for device_id in y_all]
+            uall[rows, pl.ds(pl.multiple_of(y * SUB, SUB), SUB)] = ru[3]
+            return
         outer, inner = places(m)
         rx[m, 3] = rz[m, 3, :, narrow(inner)] + rx[m, 0] + rx[m, 1] + rx[m, 2]
         span = pl.ds(pl.multiple_of(y * 2048 + outer * 512 + inner * 128, 128), 128)
@@ -414,14 +440,13 @@
         wait_all(state["yf", m][:2])
         state["yl", m] = push(fac.at[m, rows, quarter(y_opp)], other)
 
-    def f_own(m):
-        land(state["ys", m][2])
-
-    def f_near(m):
-        wait_all(state["yf", m][2:])
-
-    def f_end(m):
-        land(state["yl", m])
+    def whole(part, m):
+        if part == 0:
+            land(state["ys", m][2])
+        elif part < 3:
+            land(state["yf", m][1 + part])
+        else:
+            land(state["yl", m])
 
     def c_split(part):
         if part == 0:
@@ -436,39 +461,41 @@
 
         lax.fori_loop(part * 4, part * 4 + 4, split_pairs, 0)
 
-    up_columns = pl.multiple_of(tensor * PART, PART)
-    block = 512
     quarters = [y, y_prev, y_next, y_opp]
 
+    def merge_rows(part, t):
+        spot = pl.ds(pl.multiple_of(quarters[part] * 2048 + t * SUB, SUB), SUB)
+        return spot, pl.ds(pl.multiple_of(t * PART + quarters[part] * SUB, SUB), SUB)
+
     def c_merge_q(part):
+        wait_all(state["u"])
+        whole(part, 1)
         if part == 0:
             wq_load.wait()
 
-        def merge(i, carry):
-            ks = pl.ds(pl.multiple_of(quarters[part] * 2048 + i * block, block), block)
+        def merge(t, carry):
+            spot, ks = merge_rows(part, t)
             low = lax.dot_general(
-                fac[1, :, ks],
-                fac[0, :, pl.ds(up_columns, QW)],
-                (((0,), (0,)), ((), ())),
-                preferred_element_type=F32,
+                fac[1, :, spot], uall[:, pl.ds(0, QW)], (((0,), (0,)), ((), ())), preferred_element_type=F32
             )
             wq[ks, :] = (wq[ks, :].astype(F32) + low).astype(BF)
             return carry
 
-        lax.fori_loop(0, 4, merge, 0)
+        lax.fori_loop(0, 8, merge, 0)
 
     def c_merge_kv(part):
+        wait_all(state["u"])
+        for m in (2, 3):
+            whole(part, m)
         if part == 0:
             upkv[...] = jnp.zeros_like(upkv)
             for j in range(2):
-                upkv[pl.ds(j * RANK, RANK), pl.ds(j * KW, KW)] = fac[
-                    0, :, pl.ds(up_columns + QW + j * KW, KW)
-                ]
-
-        def merge(i, carry):
-            ks = pl.ds(pl.multiple_of(quarters[part] * 2048 + i * block, block), block)
+                upkv[pl.ds(j * RANK, RANK), pl.ds(j * KW, KW)] = uall[:, pl.ds(QW + j * KW, KW)]
+
+        def merge(t, carry):
+            spot, ks = merge_rows(part, t)
             low = lax.dot_general(
-                fac[pl.ds(2, 2), :, ks].reshape(2 * RANK, block),
+                fac[pl.ds(2, 2), :, spot].reshape(2 * RANK, SUB),
                 upkv[...],
                 (((0,), (0,)), ((), ())),
                 preferred_element_type=F32,
@@ -476,33 +503,44 @@
             mkv[ks, :] = (mkv[ks, :].astype(F32) + low).astype(BF)
             return carry
 
-        lax.fori_loop(0, 4, merge, 0)
+        lax.fori_loop(0, 8, merge, 0)
 
     sources = [
         tensor, base + z_prev, base + z_next, base + z_opp,
         far_slot, far_base + z_prev, far_base + z_next, far_base + z_opp,
     ]
 
-    def c_project(part):
-        t = sources[part]
-        if part == 0:
-            x_load.wait()
-        ks = pl.ds(pl.multiple_of(t * PART, PART), PART)
-        received = xs[t].reshape(TOK, PART)
-        query = jnp.dot(received, wq[ks, :], preferred_element_type=F32)
-        keyval = jnp.dot(received, mkv[ks, :], preferred_element_type=F32)
-        if part == 0:
+    def project(i, parts, first=False):
+        t = sources[i]
+        query = keyval = None
+        for part in parts:
+            features = pl.ds(pl.multiple_of(quarters[part] * SUB, SUB), SUB)
+            ks = pl.ds(pl.multiple_of(t * PART + quarters[part] * SUB, SUB), SUB)
+            received = xs[t, :, :, features].reshape(TOK, SUB)
+            more_query = jnp.dot(received, wq[ks, :], preferred_element_type=F32)
+            more_keyval = jnp.dot(received, mkv[ks, :], preferred_element_type=F32)
+            query = more_query if query is None else query + more_query
+            keyval = more_keyval if keyval is None else keyval + more_keyval
+        if first:
             acc[:, pl.ds(0, QW)] = query
             acc[:, pl.ds(QW, 2 * KW)] = keyval
         else:
             acc[:, pl.ds(0, QW)] += query
             acc[:, pl.ds(QW, 2 * KW)] += keyval
 
+    def c_most(i):
+        if i == 0:
+            x_load.wait()
+        project(i, (0, 1, 2), i == 0)
+
+    def c_rest(i):
+        project(i, (3,))
+
     steps = dict(
         f_core=f_core, f_second=f_second, f_third=f_third, f_ra=f_ra, f_rb=f_rb, f_sb=f_sb, f_sa=f_sa,
-        f_yf=f_yf, f_last=f_last, f_own=f_own, f_near=f_near, f_end=f_end,
+        f_yf=f_yf, f_last=f_last,
         zu=zu, zd=zd, xx=xx, x_end=x_end, c_tables=c_tables, c_split=c_split, c_merge_q=c_merge_q, c_merge_kv=c_merge_kv,
-        c_project=c_project,
+        c_most=c_most, c_rest=c_rest,
     )
     for name, index in ORDER:
         steps[name](index)
@@ -551,14 +589,17 @@
     valid = (row // 16 == lane % BLOCK) & (lane // BLOCK <= (row // 4) % 4)
     recent[...] = jnp.where(valid, scores, -1e30)
     slots = lax.broadcasted_iota(jnp.int32, (16, HD), 1)
-    for r in range(BLOCK):
+    for r in range(0, BLOCK, 2):
+        pair = pl.ds(first + r, 2)
         raw = lax.dot_general(
-            q_ref[first + r].astype(BF),
-            cache_ref[0, first + r],
+            q_ref[pair].reshape(32, HD).astype(BF),
+            cache_ref[0, pair].reshape(2 * HD, HD),
             (((1,), (1,)), ((), ())),
             preferred_element_type=F32,
         )
-        q_ref[first + r] = jnp.where(slots < len_ref[first + r], raw * scale, -1e30)
+        for j in range(2):
+            mine = raw[16 * j : 16 * j + 16, HD * j : HD * j + HD]
+            q_ref[first + r + j] = jnp.where(slots < len_ref[first + r + j], mine * scale, -1e30)
     for part in range(4):
         group = pl.ds(first + part * BLOCK // 4, BLOCK // 4)
         mine = pl.ds(part * BLOCK * 4, BLOCK * 4)
@@ -570,10 +611,11 @@
         total = jnp.sum(cached + fresh, axis=1, keepdims=True)
         recent_probs[mine, :] = (fresh / total).astype(BF)
         probs[mine, :] = (cached / total).astype(BF)
-    for r in range(BLOCK):
-        q_ref[first + r] = jnp.dot(
-            probs[pl.ds(r * 16, 16), :], cache_ref[1, first + r], preferred_element_type=F32
-        )
+    for r in range(0, BLOCK, 2):
+        both = jnp.concatenate([cache_ref[1, first + r], cache_ref[1, first + r + 1]], axis=1)
+        raw = jnp.dot(probs[pl.ds(r * 16, 32), :], both, preferred_element_type=F32)
+        for j in range(2):
+            q_ref[first + r + j] = raw[16 * j : 16 * j + 16, HD * j : HD * j + HD]
     values = v_ref[:, rows, :].reshape(BLOCK * STEPS, HD)
     q_ref[rows] += jnp.dot(recent_probs[...], values, preferred_element_type=F32).reshape(
         BLOCK, 16, HD
@@ -619,11 +661,14 @@
             pltpu.VMEM((RANK, D), BF),
             pltpu.VMEM((3, HALF, D), BF),
             pltpu.VMEM((4, HALF, D), BF),
+            pltpu.VMEM((4, HALF, D), BF),
             pltpu.VMEM((4, 6, HALF // 2, 2048), BF),
             pltpu.VMEM((4, HALF, 2048), BF),
             pltpu.VMEM((4, 4, HALF, 512), BF),
             pltpu.VMEM((4, 4, HALF, 128), BF),
             pltpu.VMEM((4, RANK, D), BF),
+            pltpu.VMEM((4, HALF, SUB), BF),
+            pltpu.VMEM((RANK, PART), BF),
             pltpu.VMEM((2 * RANK, 2 * KW), BF),
             pltpu.VMEM((TOK, QW + 2 * KW), F32),
             pltpu.VMEM((TOK, HD), F32),

time: 94.8 us -> 86.6 us (0.914)
  Pallas kernels: 92.7 us -> 84.6 us
    pallas_call x1, Pallas kernels: 92.7 us -> 84.6 us  [body(): pl.pallas_call(decode, out_shape=jax.ShapeDtypeStruct((STEPS, ROWS, QW),...]
where the time goes in v3:
time: 86.6 us; the launch traced here: 86.5 us
  Pallas kernels  84.6 us (98%)
  local copies, waits for them, and re-layouts  1.87 us (2%)
    pallas_call x1, Pallas kernels, body(): pl.pallas_call(decode, out_shape=jax.ShapeDtypeStruct((STEPS, ROWS, QW),...  84.6 us
    unnamed x1, local copies, waits for them, and re-layouts  1.87 us

profile of v3, /device:TPU:1, one launch (start us, length us, event | category | flops | bytes accessed | tf_op | source)
XLA Modules:
  0.0 86.5 jit_solution(7845753756534877013)
XLA Ops:
  0.0 84.6 %shard_map.100 = bf16[4,128,512]{2,1,0:T(8,128)(2,1)} custom-call(s32[3]{0:T(128)} %owners_ref.1, bf16[4,128,1024]{2,1,0:T(8,128)(2,1)} %x_hbm.1, bf16[8192,512]{1,0:T(8,128)(2,1)} %wq_hbm.1, bf16[16384,128]{1,0:T(8,128)(2,1)} %bitcast.3, bf16[1,3,64,8192]{3,2,1,0:T(8,128)(2,1)} %down_hbm.1, bf16[1,64,6144]{2,1,0:T(8,128)(2,1)} %up_hbm.1, f32[1,512]{1,0:T(1,128)} %bitcast.5, ...), custom_call_target="tpu_custom_call" | custom-call | tf_op jit(solution)/shard_map/pallas_call | solution.py:643
  84.6 1.9 %copy.12 = bf16[4,128,512]{2,1,0:T(8,128)(2,1)} copy(bf16[4,128,512]{2,1,0:T(8,128)(2,1)} %shard_map.100) | data formatting | bytes 1048576
